TPU v7x, 512 devices: a whole 4x4x16 slice. The times are simulated.
512 devices in a mesh: grp: 16 (over y, x_hi, core), proto: 32 (over x_lo, z).
Axes of the slice: x: 4 (x_hi: 2, x_lo: 2; x = x_hi * 2 + x_lo), y: 4, z: 16, core: 2. Of those that a mesh axis runs over, the one named last changes fastest.
Arguments:
- teacher_features: bfloat16 [8192, 256], P('grp'), may hold values from -0.65 to 0.65
- student_features: bfloat16 [8192, 256], P('grp'), may hold values from -0.65 to 0.65
- prototypes: bfloat16 [256, 131072], P(None, 'proto'), may hold values from -0.65 to 0.65
Outputs:
- proto_grad: bfloat16 [256, 131072], P('grp', 'proto')
- student_grad: bfloat16 [8192, 256], P('grp')
- mean_loss: float32 [], replicated
All inputs are finite; a program needn't handle non-finite values.
Results may differ from a plain program's by a relative error of at most 0.0043.
Values may be sent and summed in bfloat16 or wider, within the bound.
A program may use at most 64 MiB of HBM per device.

v0:
```python
import jax
import jax.numpy as jnp
from jax import lax
from jax.sharding import PartitionSpec as P

ITERS = 3


teacher_temp = 0.07
student_temp = 0.1
epsilon = 1e-06
highest = lax.Precision.HIGHEST


def unit_rows(features):
    float_rows = features.astype(jnp.float32)
    scaling = lax.rsqrt(jnp.sum(float_rows * float_rows, axis=1, keepdims=True) + epsilon)
    return (float_rows * scaling, scaling)


def column_totals(row_scale, exps):
    local_mass = jnp.dot(row_scale, exps, precision=highest)
    return lax.psum(local_mass, "grp")


def row_totals(exps, col_scale):
    local_mass = jnp.dot(exps, col_scale, precision=highest)
    return lax.psum(local_mass, "proto")


def per_device(teacher_features, student_features, prototypes):
    groups = lax.axis_size("grp")
    rows_here, bottleneck = student_features.shape
    columns_here = prototypes.shape[1]
    all_rows = rows_here * groups
    all_protos = columns_here * lax.axis_size("proto")
    teacher_wide, teacher_scaling = unit_rows(teacher_features)
    teacher_unit = teacher_wide.astype(jnp.bfloat16)
    student_wide, student_scaling = unit_rows(student_features)
    student_unit = student_wide.astype(jnp.bfloat16)
    proto_float = prototypes.astype(jnp.float32)
    proto_scaling = lax.rsqrt(jnp.sum(proto_float * proto_float, axis=0, keepdims=True) + epsilon)
    proto_wide = proto_float * proto_scaling
    proto_unit = proto_wide.astype(jnp.bfloat16)
    exps = jnp.exp(
        jnp.dot(teacher_unit, proto_unit, preferred_element_type=jnp.float32) / teacher_temp
    )
    row_scale = jnp.ones((rows_here,), jnp.float32)
    col_scale = jnp.ones((columns_here,), jnp.float32)
    for iteration in range(ITERS):
        col_scale = 1.0 / (all_protos * column_totals(row_scale, exps))
        row_scale = 1.0 / (all_rows * row_totals(exps, col_scale))
    targets = all_rows * exps * row_scale[:, None] * col_scale[None, :]
    logits = jnp.dot(student_unit, proto_unit, preferred_element_type=jnp.float32) / student_temp
    student_total = lax.psum(jnp.sum(jnp.exp(logits), axis=1), "proto")
    log_probs = logits - jnp.log(student_total)[:, None]
    probabilities = jnp.exp(log_probs)
    loss_local = -jnp.sum(targets * log_probs)
    mean_loss = lax.psum(loss_local, ("grp", "proto")) / all_rows
    dlogits = ((probabilities - targets) / student_temp).astype(jnp.bfloat16)
    local_unit = lax.dot_general(
        dlogits, proto_unit, (((1,), (1,)), ((), ())), preferred_element_type=jnp.float32
    )
    unit_grad = lax.psum(local_unit, "proto")
    row_dots = jnp.sum(student_wide * unit_grad, axis=1, keepdims=True)
    student_grad = ((unit_grad - student_wide * row_dots) * student_scaling).astype(jnp.bfloat16)
    position = lax.axis_index("grp")
    row_share = bottleneck // groups
    reduced_rows = lax.psum_scatter(
        lax.dot_general(
            student_unit, dlogits, (((0,), (0,)), ((), ())), preferred_element_type=jnp.float32
        ),
        "grp",
        scatter_dimension=0,
        tiled=True,
    )
    proto_rows = lax.dynamic_slice_in_dim(proto_wide, position * row_share, row_share, 0)
    column_dots = lax.psum(jnp.sum(proto_rows * reduced_rows, axis=0), "grp")
    proto_grad = ((reduced_rows - proto_rows * column_dots[None, :]) * proto_scaling).astype(
        jnp.bfloat16
    )
    return (proto_grad, student_grad, mean_loss)


def solution(mesh):
    placed = (P("grp", None), P("grp", None), P(None, "proto"))
    return jax.shard_map(
        per_device,
        mesh=mesh,
        in_specs=placed,
        out_specs=(P("grp", "proto"), P("grp", None), P()),
        check_vma=False,
    )
```

profile of v0, /device:TPU:1, one launch (start us, length us, event | category | flops | bytes accessed | tf_op | source)
XLA Modules:
  0.0 790.8 jit_solution(13892264253493831751)
XLA Ops:
  8.0 0.0 all-reduce.3.cloned.1.call-start
  8.0 2.0 fusion
  10.1 1.1 fusion.15
  11.2 3.2 multiply_exponential_fusion
  14.4 0.0 copy-start
  14.4 3.2 copy-done
  17.6 4.0 fusion.22
  21.6 65.9 %psum.71 = f32[4096]{0:T(1024)S(1)} all-reduce(f32[4096]{0:T(1024)S(1)} %bitcast.29), channel_id=1, replica_groups=mesh['grp'=16,'proto'=32] {'grp'}, use_global_device_ids=true, to_apply=%region_5.0 | all-reduce | flops 4096 | bytes 32768 | tf_op jit(solution)/shard_map/psum | solution.py:23
  87.5 9.4 %fusion.25 = f32[1,512]{1,0:T(1,128)S(1)} fusion(f32[512,4096]{1,0:T(8,128)} %copy-done, f32[4096,1]{0,1:T(1,128)S(1)} %bitcast.25), kind=kOutput, calls=%fused_computation.41 | convolution fusion | flops 25165824 | bytes 8407040 | tf_op jit(solution)/shard_map/dot_general | solution.py:27
  97.0 54.8 %psum.72 = f32[512]{0:T(512)S(1)} all-reduce(f32[512]{0:T(512)S(1)} %bitcast.31), channel_id=1, replica_groups=mesh['grp'=16,'proto'=32] {'proto'}, use_global_device_ids=true, to_apply=%region_6.0 | all-reduce | flops 512 | bytes 4096 | tf_op jit(solution)/shard_map/psum | solution.py:28
  151.8 6.3 fusion.26
  158.2 79.1 %psum.73 = f32[4096]{0:T(1024)S(1)} all-reduce(f32[4096]{0:T(1024)S(1)} %bitcast.26), channel_id=1, replica_groups=mesh['grp'=16,'proto'=32] {'grp'}, use_global_device_ids=true, to_apply=%region_7.0 | all-reduce | flops 4096 | bytes 32768 | tf_op jit(solution)/shard_map/psum | solution.py:23
  237.3 9.4 %fusion.27 = f32[1,512]{1,0:T(1,128)S(1)} fusion(f32[512,4096]{1,0:T(8,128)} %copy-done, f32[4096,1]{0,1:T(1,128)S(1)} %bitcast.27), kind=kOutput, calls=%fused_computation.43 | convolution fusion | flops 25165824 | bytes 8407040 | tf_op jit(solution)/shard_map/dot_general | solution.py:27
  246.7 46.1 %psum.74 = f32[512]{0:T(512)S(1)} all-reduce(f32[512]{0:T(512)S(1)} %bitcast.33), channel_id=1, replica_groups=mesh['grp'=16,'proto'=32] {'proto'}, use_global_device_ids=true, to_apply=%region_8.0 | all-reduce | flops 512 | bytes 4096 | tf_op jit(solution)/shard_map/psum | solution.py:28
  292.8 0.0 copy-start.3
  292.8 0.0 copy-start.1
  292.8 6.5 fusion.28
  299.3 79.0 %psum.75 = f32[4096]{0:T(1024)S(1)} all-reduce(f32[4096]{0:T(1024)S(1)} %bitcast.28), channel_id=1, replica_groups=mesh['grp'=16,'proto'=32] {'grp'}, use_global_device_ids=true, to_apply=%region_9.0 | all-reduce | flops 4096 | bytes 32768 | tf_op jit(solution)/shard_map/psum | solution.py:23
  378.3 9.4 %fusion.29 = f32[1,512]{1,0:T(1,128)S(1)} fusion(f32[512,4096]{1,0:T(8,128)} %copy-done, f32[4096,1]{0,1:T(1,128)S(1)} %bitcast.24), kind=kOutput, calls=%fused_computation.45 | convolution fusion | flops 25165824 | bytes 8407040 | tf_op jit(solution)/shard_map/dot_general | solution.py:27
  387.7 0.0 copy-done.3
  387.8 0.1 fusion.14
  387.9 0.0 copy-done.1
  387.9 4.9 exponential_reduce_fusion
  392.9 47.8 %all-reduce = (f32[512]{0:T(512)S(1)}, f32[512]{0:T(512)S(1)}) all-reduce(f32[512]{0:T(512)S(1)} %bitcast.30, f32[512]{0:T(512)S(1)} %get-tuple-element.7), channel_id=1, replica_groups=mesh['grp'=16,'proto'=32] {'proto'}, use_global_device_ids=true, to_apply=%region_10.0 | all-reduce | flops 1024 | bytes 8192 | tf_op jit(solution)/shard_map/psum | solution.py:28
  440.7 8.2 %multiply_reduce_fusion = (f32[]{:T(128)}, bf16[512,4096]{1,0:T(8,128)(2,1)S(1)}) fusion(f32[512,4096]{1,0:T(8,128)} %copy-done, f32[512,4096]{1,0:T(8,128)} %get-tuple-element.8, f32[4096]{0:T(1024)S(1)} %multiply_divide_fusion, f32[512]{0:T(512)S(1)} %divide_multiply_fusion, f32[512]{0:T(512)S(1)} %log.3), kind=kLoop, calls=%fused_computation | loop fusion | flops 18874368 | bytes 20992004 | tf_op jit(solution)/shard_map/reduce_sum | solution.py:58
  448.9 0.0 copy-start.2
  448.9 2.0 copy-done.2
  450.8 2.3 fusion.2
  453.1 0.0 all-reduce.3.cloned.1.call-update
  453.1 0.0 reduce-scatter.2.cloned.1.call-start
  453.2 5.5 fusion.19
  458.7 0.0 reduce-scatter.2.cloned.1.call-update
  459.3 118.3 %psum.79 = f32[]{:T(128)} all-reduce(f32[]{:T(128)S(6)} %neg.3), channel_id=1, replica_groups=mesh['grp'=16,'proto'=32] {'grp','proto'}, use_global_device_ids=true, to_apply=%region_17.0 | all-reduce | flops 1 | bytes 8 | tf_op jit(solution)/shard_map/psum | solution.py:59
  578.2 2.5 convert_multiply_fusion
  580.7 114.1 %all-reduce.3.cloned.1.call-done = f32[512,256]{1,0:T(8,128)} async-done(((f32[512,256]{1,0:T(8,128)}), f32[512,256]{1,0:T(8,128)}) %all-reduce.3.cloned.1.call-update) | async-done | bytes 524304 | tf_op jit(solution)/shard_map/psum | solution.py:64
  694.8 1.3 fusion.10
  696.1 2.0 fusion.13
  698.0 0.0 reduce-scatter.2.cloned.1.call-done
  698.1 1.1 multiply_reduce_fusion.1
  699.1 81.4 %psum.77 = f32[4096]{0:T(1024)S(1)} all-reduce(f32[4096]{0:T(1024)S(1)} %multiply_reduce_fusion.1), channel_id=1, replica_groups=mesh['grp'=16,'proto'=32] {'grp'}, use_global_device_ids=true, to_apply=%region_13.0 | all-reduce | flops 4096 | bytes 32768 | tf_op jit(solution)/shard_map/psum | solution.py:78
  780.5 1.7 multiply_convert_fusion.1
  (10 shorter events, 0.1 us)
Async XLA Ops:
  8.0 686.8 %all-reduce.3.cloned.1.call-start = ((), (), s32[]{:S(2)}) async-start(), calls=%async_computation.2 | async-start | bytes 1048576 | tf_op jit(solution)/shard_map/psum | solution.py:64
  14.4 3.2 copy-start
  292.8 94.9 %copy-start.3 = (bf16[512,256]{1,0:T(8,128)(2,1)S(1)}, bf16[512,256]{1,0:T(8,128)(2,1)}, u32[]{:S(2)}) copy-start(bf16[512,256]{1,0:T(8,128)(2,1)} %param.4) | copy-start | bytes 786436
  292.8 95.1 %copy-start.1 = (bf16[256,4096]{1,0:T(8,128)(2,1)S(1)}, bf16[256,4096]{1,0:T(8,128)(2,1)}, u32[]{:S(2)}) copy-start(bf16[256,4096]{1,0:T(8,128)(2,1)} %param.5) | copy-start | bytes 6291460
  448.9 2.0 copy-start.2
  453.1 244.9 %reduce-scatter.2.cloned.1.call-start = ((), (), s32[]{:S(2)}) async-start(), calls=%async_computation.1 | async-start | bytes 4456448 | tf_op jit(solution)/shard_map/reduce_scatter | solution.py:69
Sparse Core Ops, SparseCore 0:
  453.2 241.5 all-reduce.2
Sparse Core Ops, SparseCore 1:
  458.8 108.5 reduce-scatter.1
where the time goes:
time: 795 us; the launch traced here: 791 us
  blocking collectives  572 us (72%)
  waiting for transfers between devices  114 us (14%)
  matrix products  61 us (8%)
  other arithmetic  20 us (3%)
  between operations  18 us (2%)
    psum x3, blocking collectives, column_totals(): return lax.psum(local_mass, 'grp')  224 us
    psum x3, blocking collectives, row_totals(): return lax.psum(local_mass, 'proto')  149 us
    psum x1, blocking collectives, per_device(): mean_loss = lax.psum(loss_local, ('grp', 'proto')) / all_rows  118 us
    psum x1, waiting for transfers between devices, per_device(): unit_grad = lax.psum(local_unit, 'proto')  114 us
    psum x1, blocking collectives, per_device(): column_dots = lax.psum(jnp.sum(proto_rows * reduced_rows, axis=0), 'grp')  81.4 us
    dot_general x3, matrix products, row_totals(): local_mass = jnp.dot(exps, col_scale, precision=highest)  28.3 us
    dot_general x3, matrix products, column_totals(): local_mass = jnp.dot(row_scale, exps, precision=highest)  16.9 us
  transfers between devices with their start and end apart: 2, of which 1 were waited for; matrix products, arithmetic and copies ran while one was open for 1% of the time, Pallas kernels for 0%

commit v1 on v0

v1 whole, which is shorter than its diff:
```python
import functools
import math

import jax
import jax.numpy as jnp
from jax import lax
from jax.experimental import pallas as pl
from jax.experimental.pallas import tpu as pltpu
from jax.sharding import PartitionSpec as P

MESH = pl.DeviceIdType.MESH
F32 = jnp.float32
BF16 = jnp.bfloat16

ITERS = 3
TEACHER_TEMP = 0.07
STUDENT_TEMP = 0.1
EPSILON = 1e-06
LOG2E = math.log2(math.e)

ROWS = 512
COLS = 4096
WIDTH = 256
GRP = 16
RING = 16
ALL_ROWS = ROWS * GRP
ALL_COLS = COLS * 2 * RING
BLOCK = 512
BLOCKS = COLS // BLOCK
TILES = COLS // 128
SHARE = WIDTH // GRP
CHIPS = 8
OWN = ROWS // (2 * RING)


def lane_broadcast(vector):
    parts = []
    for group in range(4):
        parts.append(jnp.broadcast_to(vector[group : group + 1, :], (128, 128)).T)
    return jnp.concatenate(parts, axis=0)


def fold_lanes(partial):
    parts = []
    for group in range(4):
        block = partial[group * 128 : (group + 1) * 128, :].T
        parts.append(jnp.sum(block, axis=0, keepdims=True))
    return jnp.concatenate(parts, axis=0)


def kernel(
    teacher_hbm,
    student_hbm,
    proto_hbm,
    proto_out,
    student_out,
    loss_out,
    teacher_in,
    student_in,
    proto_in,
    student_unit,
    student_turned,
    proto_unit,
    proto_scale,
    exps,
    soft,
    half,
    row_wide,
    col_sums,
    col_send,
    col_recv,
    col_scale,
    row_send,
    row_pair,
    row_recv,
    unit_part,
    unit_send,
    unit_pair,
    unit_share,
    unit_mine,
    unit_recv,
    term,
    core_send,
    core_recv,
    term_mine,
    term_send,
    term_recv,
    dots,
    dot_send,
    dot_recv,
    in_sem,
    col_ss,
    col_rs,
    rowx_ss,
    rowx_rs,
    rowz_ss,
    rowz_rs,
    unitx_ss,
    unitx_rs,
    unitz_ss,
    unitz_rs,
    outz_ss,
    outz_rs,
    outx_ss,
    outx_rs,
    core_ss,
    core_rs,
    term_ss,
    term_rs,
    dot_ss,
    dot_rs,
):
    grp = lax.axis_index("grp")
    proto = lax.axis_index("proto")
    core = lax.rem(grp, 2)
    chip = lax.div(grp, 2)
    x_lo = lax.div(proto, RING)
    z = lax.rem(proto, RING)
    partner_core = (grp + 1 - 2 * core, proto)
    partner_x = (grp, z + (1 - x_lo) * RING)

    def grp_peer(step):
        return lax.rem(grp + step, GRP)

    def z_peer(step):
        return lax.rem(z + step, RING)

    def chip_peer(step):
        return lax.rem(chip + step, CHIPS)

    def remote(src, dst, send, recv, device):
        return pltpu.make_async_remote_copy(
            src_ref=src, dst_ref=dst, send_sem=send, recv_sem=recv, device_id=device, device_id_type=MESH
        )

    barrier = pltpu.get_barrier_semaphore()

    def greet_grp(step, carry):
        pl.semaphore_signal(barrier, inc=1, device_id=(grp_peer(step), proto), device_id_type=MESH)
        return carry

    def greet_z(step, carry):
        pl.semaphore_signal(barrier, inc=1, device_id=(grp, x_lo * RING + z_peer(step)), device_id_type=MESH)
        return carry

    lax.fori_loop(1, RING, greet_z, 0)
    lax.fori_loop(1, GRP, greet_grp, 0)
    pl.semaphore_signal(barrier, inc=1, device_id=partner_x, device_id_type=MESH)

    loads = [
        pltpu.make_async_copy(teacher_hbm, teacher_in, in_sem.at[0]),
        pltpu.make_async_copy(student_hbm, student_in, in_sem.at[1]),
        pltpu.make_async_copy(proto_hbm, proto_in, in_sem.at[2]),
    ]
    for load in loads:
        load.start()

    def unit_rows(features):
        wide = features.astype(F32)
        scaling = lax.rsqrt(jnp.sum(wide * wide, axis=1, keepdims=True) + EPSILON)
        return wide * scaling, scaling

    loads[0].wait()
    loads[1].wait()
    teacher_in[...] = unit_rows(teacher_in[...])[0].astype(BF16)
    student_unit[...] = unit_rows(student_in[...])[0].astype(BF16)
    loads[2].wait()

    def columns(block):
        return pl.ds(pl.multiple_of(block * BLOCK, BLOCK), BLOCK)

    def teacher_block(block, carry):
        cols = columns(block)
        wide = proto_in[:, cols].astype(F32)
        scaling = lax.rsqrt(jnp.sum(wide * wide, axis=0, keepdims=True) + EPSILON)
        proto_scale[:, cols] = scaling
        unit = (wide * scaling).astype(BF16)
        proto_unit[:, cols] = unit
        product = jnp.dot(teacher_in[...], unit, preferred_element_type=F32)
        values = jnp.exp2(product * (LOG2E / TEACHER_TEMP))
        exps[:, cols] = values
        total = jnp.sum(values, axis=0, keepdims=True)
        for tile in range(BLOCK // 128):
            col_sums[pl.ds(block * (BLOCK // 128) + tile, 1), :] = total[:, tile * 128 : (tile + 1) * 128]
        return carry

    lax.fori_loop(0, BLOCKS, teacher_block, 0)

    pl.semaphore_wait(barrier, GRP - 1 + RING - 1 + 1)

    def col_copy(turn, step):
        peer = grp_peer(step)
        return remote(
            col_send.at[turn], col_recv.at[turn, grp], col_ss.at[turn, step], col_rs.at[turn, grp], (peer, proto)
        )

    def col_start(turn):
        col_send[turn] = col_sums[...].astype(BF16)
        col_recv[turn, grp] = col_sums[...].astype(BF16)
        lax.fori_loop(1, GRP, lambda step, carry: (col_copy(turn, step).start(), carry)[1], 0)

    def col_finish(turn):
        def wait(step, carry):
            peer = grp_peer(step)
            remote(
                col_send.at[turn], col_recv.at[turn, peer], col_ss.at[turn, step], col_rs.at[turn, peer], (peer, proto)
            ).wait()
            return carry

        lax.fori_loop(1, GRP, wait, 0)
        total = col_recv[turn, 0].astype(F32)
        for peer in range(1, GRP):
            total = total + col_recv[turn, peer].astype(F32)
        col_scale[...] = 1.0 / (ALL_COLS * total)

    def row_start(turn):
        rows = pl.ds(0, 4 if turn == 1 else 8)
        copy = remote(
            row_send.at[turn, rows], row_pair.at[turn, rows], rowx_ss.at[turn], rowx_rs.at[turn], partner_x
        )
        copy.start()
        return copy

    def row_ring(turn, copy):
        size = 4 if turn == 1 else 8
        rows = pl.ds(0, size)
        copy.wait()
        total = row_send[turn, rows] + row_pair[turn, rows]
        row_send[turn, rows] = total
        row_recv[turn, z, rows] = total

        def send(step, carry):
            peer = z_peer(step)
            remote(
                row_send.at[turn, rows],
                row_recv.at[turn, z, rows],
                rowz_ss.at[turn, step],
                rowz_rs.at[turn, z],
                (grp, x_lo * RING + peer),
            ).start()
            return carry

        lax.fori_loop(1, RING, send, 0)

    def row_finish(turn):
        size = 4 if turn == 1 else 8
        rows = pl.ds(0, size)

        def wait(step, carry):
            peer = z_peer(step)
            remote(
                row_send.at[turn, rows],
                row_recv.at[turn, peer, rows],
                rowz_ss.at[turn, step],
                rowz_rs.at[turn, peer],
                (grp, x_lo * RING + peer),
            ).wait()
            return carry

        lax.fori_loop(1, RING, wait, 0)
        total = row_recv[turn, 0, rows]
        for peer in range(1, RING):
            total = total + row_recv[turn, peer, rows]
        return total

    def row_pass(last):
        def rows_of(block, carry):
            rows = pl.ds(pl.multiple_of(block * 64, 64), 64)
            partial = jnp.zeros((64, 128), F32)
            for tile in range(TILES):
                cols = pl.ds(tile * 128, 128)
                scaled = exps[rows, cols] * col_scale[pl.ds(tile, 1), :]
                if last:
                    exps[rows, cols] = scaled
                    half[rows, cols] = scaled.astype(BF16)
                partial = partial + scaled
            row_wide[rows, :] = partial
            return carry

        lax.fori_loop(0, ROWS // 64, rows_of, 0)
        return fold_lanes(row_wide[...])

    def col_pass():
        def block_of(block, carry):
            cols = columns(block)
            partial = jnp.zeros((8, BLOCK), F32)
            for group in range(ROWS // 8):
                rows = pl.ds(group * 8, 8)
                scale = row_wide[rows, :]
                partial = partial + exps[rows, cols] * jnp.concatenate([scale] * (BLOCK // 128), axis=1)
            total = jnp.sum(partial, axis=0, keepdims=True)
            for tile in range(BLOCK // 128):
                col_sums[pl.ds(block * (BLOCK // 128) + tile, 1), :] = total[:, tile * 128 : (tile + 1) * 128]
            return carry

        lax.fori_loop(0, BLOCKS, block_of, 0)

    def unit_matmul():
        unit_part[...] = lax.dot_general(
            half[...], proto_unit[...], (((1,), (1,)), ((), ())), preferred_element_type=F32
        )

    half_rows = ROWS // 2

    def unit_start(part):
        unit_send[part] = unit_part[pl.ds(pl.multiple_of((1 - x_lo) * half_rows, half_rows), half_rows), :].astype(BF16)
        unit_mine[part] = unit_part[pl.ds(pl.multiple_of(x_lo * half_rows, half_rows), half_rows), :]
        copy = remote(unit_send.at[part], unit_pair.at[part], unitx_ss.at[part], unitx_rs.at[part], partner_x)
        copy.start()
        return copy

    def own_rows(index):
        return pl.ds(pl.multiple_of(index * OWN, OWN), OWN)

    def unit_ring(part, copy):
        copy.wait()
        total = unit_mine[part] + unit_pair[part].astype(F32)
        unit_mine[part] = total
        unit_share[part] = total.astype(BF16)

        def send(step, carry):
            peer = z_peer(step)
            remote(
                unit_share.at[part, own_rows(peer)],
                unit_recv.at[part, z],
                unitz_ss.at[part, step],
                unitz_rs.at[part, z],
                (grp, x_lo * RING + peer),
            ).start()
            return carry

        lax.fori_loop(1, RING, send, 0)

    def unit_finish(part):
        def wait(step, total):
            peer = z_peer(step)
            remote(
                unit_share.at[part, own_rows(peer)],
                unit_recv.at[part, peer],
                unitz_ss.at[part, step],
                unitz_rs.at[part, peer],
                (grp, x_lo * RING + peer),
            ).wait()
            return total + unit_recv[part, peer].astype(F32)

        return lax.fori_loop(1, RING, wait, unit_mine[part, own_rows(z), :])

    col_start(0)

    def student_block(block, carry):
        cols = columns(block)
        product = jnp.dot(student_unit[...], proto_unit[:, cols], preferred_element_type=F32)
        values = jnp.exp2(product * (LOG2E / STUDENT_TEMP))
        soft[:, cols] = values
        partial = values[:, :128]
        for tile in range(1, BLOCK // 128):
            partial = partial + values[:, tile * 128 : (tile + 1) * 128]
        row_wide[...] = row_wide[...] + partial
        return carry

    row_wide[...] = jnp.zeros((ROWS, 128), F32)
    lax.fori_loop(0, BLOCKS, student_block, 0)
    row_send[0, 4:8] = fold_lanes(row_wide[...])
    col_finish(0)
    row_send[0, 0:4] = row_pass(False)
    copy = row_start(0)
    row_ring(0, copy)
    sums = row_finish(0)
    row_scale = 1.0 / (ALL_ROWS * sums[0:4])
    student_total = sums[4:8]

    row_wide[...] = lane_broadcast(row_scale)
    col_pass()
    col_start(1)
    row_wide[...] = lane_broadcast((1.0 / STUDENT_TEMP) / student_total)

    def soft_rows(block, carry):
        rows = pl.ds(pl.multiple_of(block * 64, 64), 64)
        scale = row_wide[rows, :]
        for tile in range(TILES):
            cols = pl.ds(tile * 128, 128)
            scaled = soft[rows, cols] * scale
            soft[rows, cols] = scaled
            half[rows, cols] = scaled.astype(BF16)
        return carry

    lax.fori_loop(0, ROWS // 64, soft_rows, 0)
    unit_matmul()
    unit_copy = unit_start(0)
    col_finish(1)
    row_send[1, 0:4] = row_pass(False)
    copy = row_start(1)
    row_ring(1, copy)
    student_turned[...] = student_unit[...].astype(F32).T.astype(BF16)
    row_scale = 1.0 / (ALL_ROWS * row_finish(1))

    row_wide[...] = lane_broadcast(row_scale)
    col_pass()
    col_start(2)
    unit_ring(0, unit_copy)
    col_finish(2)
    row_send[2, 0:4] = row_pass(True)
    unit_matmul()
    row_wide[...] = unit_part[:, :128] * student_unit[:, :128].astype(F32) + unit_part[:, 128:] * student_unit[
        :, 128:
    ].astype(F32)
    row_send[2, 4:8] = fold_lanes(row_wide[...])
    copy = row_start(2)
    unit_copy = unit_start(1)
    row_ring(2, copy)
    unit_ring(1, unit_copy)
    soft_unit = unit_finish(0)
    sums = row_finish(2)
    row_scale = 1.0 / (ALL_ROWS * sums[0:4])
    agreement = (ALL_ROWS / STUDENT_TEMP) * row_scale * sums[4:8]
    loss_here = jnp.sum(jnp.log(student_total) - agreement) * (1.0 / ALL_ROWS)
    row_wide[...] = lane_broadcast((ALL_ROWS / STUDENT_TEMP) * row_scale)

    def core_copy(block):
        return remote(core_send.at[block], core_recv.at[block], core_ss.at[block], core_rs.at[block], partner_core)

    def term_ring(block):
        core_copy(block).wait()
        total = term_mine[block] + core_recv[block].astype(F32)
        term_mine[block] = total
        term_send[block] = total.astype(BF16)

        def send(step, carry):
            peer = chip_peer(step)
            remote(
                term_send.at[block, peer],
                term_recv.at[block, chip],
                term_ss.at[block, step],
                term_rs.at[block, chip],
                (peer * 2 + core, proto),
            ).start()
            return carry

        lax.fori_loop(1, CHIPS, send, 0)

    def term_block(block, carry):
        cols = columns(block)
        scale = row_wide[...]

        wide_scale = jnp.concatenate([scale] * (BLOCK // 128), axis=1)
        half[:, cols] = (soft[:, cols] - exps[:, cols] * wide_scale).astype(BF16)
        product = jnp.dot(student_turned[...], half[:, cols], preferred_element_type=F32)
        total = jnp.sum(product * proto_in[:, cols].astype(F32), axis=0, keepdims=True) * proto_scale[:, cols]
        for tile in range(BLOCK // 128):
            dots[pl.ds(block * (BLOCK // 128) + tile, 1), :] = total[:, tile * 128 : (tile + 1) * 128]
        term[...] = product.reshape(CHIPS, 2, SHARE, BLOCK)
        core_send[block] = term[:, 1 - core].astype(BF16)
        term_mine[block] = term[:, core]
        core_copy(block).start()

        @pl.when(block > 0)
        def _():
            term_ring(block - 1)

        return carry

    lax.fori_loop(0, BLOCKS, term_block, 0)
    term_ring(BLOCKS - 1)

    high = loss_here.astype(BF16).astype(F32)
    middle = (loss_here - high).astype(BF16).astype(F32)
    low = loss_here - high - middle
    place = lax.broadcasted_iota(jnp.int32, (16, 128), 0)
    pieces = jnp.where(place == 0, high, jnp.where(place == 1, middle, jnp.where(place == 2, low, 0.0)))
    dot_send[0:TILES] = dots[...].astype(BF16)
    dot_send[TILES : TILES + 16] = pieces.astype(BF16)
    dot_recv[grp] = dot_send[...]

    def dot_start(step, carry):
        peer = grp_peer(step)
        remote(dot_send, dot_recv.at[grp], dot_ss.at[step], dot_rs.at[grp], (peer, proto)).start()
        return carry

    lax.fori_loop(1, GRP, dot_start, 0)

    target_unit = unit_finish(1)
    my_rows = own_rows(x_lo * RING + z)
    unit_grad = soft_unit - target_unit * row_wide[my_rows, 0:1]
    wide, scaling = unit_rows(student_in[my_rows, :])
    row_dots = jnp.sum(wide * unit_grad, axis=1, keepdims=True)
    student_out[my_rows, :] = ((unit_grad - wide * row_dots) * scaling).astype(BF16)

    def out_copy(step, owner):
        peer = z_peer(step)
        rows = own_rows(x_lo * RING + owner)
        return remote(
            student_out.at[rows],
            student_out.at[rows],
            outz_ss.at[step],
            outz_rs.at[owner],
            (grp, x_lo * RING + peer),
        )

    lax.fori_loop(1, RING, lambda step, carry: (out_copy(step, z).start(), carry)[1], 0)

    def dot_wait(step, carry):
        peer = grp_peer(step)
        remote(dot_send, dot_recv.at[peer], dot_ss.at[step], dot_rs.at[peer], (peer, proto)).wait()
        return carry

    lax.fori_loop(1, GRP, dot_wait, 0)
    total = dot_recv[0].astype(F32)
    for peer in range(1, GRP):
        total = total + dot_recv[peer].astype(F32)
    dots[...] = total[0:TILES]
    loss_out[...] = total[TILES : TILES + 1] + total[TILES + 1 : TILES + 2] + total[TILES + 2 : TILES + 3]

    def term_finish(block, carry):
        cols = columns(block)

        def wait(step, total):
            peer = chip_peer(step)
            remote(
                term_send.at[block, peer],
                term_recv.at[block, peer],
                term_ss.at[block, step],
                term_rs.at[block, peer],
                (peer * 2 + core, proto),
            ).wait()
            return total + term_recv[block, peer].astype(F32)

        total = lax.fori_loop(1, CHIPS, wait, term_mine[block, chip])
        scaling = proto_scale[:, cols]
        wide = proto_in[pl.ds(pl.multiple_of(grp * SHARE, SHARE), SHARE), cols].astype(F32) * scaling
        dot = jnp.concatenate(
            [dots[pl.ds(block * (BLOCK // 128) + tile, 1), :] for tile in range(BLOCK // 128)], axis=1
        )
        proto_out[:, cols] = ((total - wide * dot) * scaling).astype(BF16)
        return carry

    lax.fori_loop(0, BLOCKS, term_finish, 0)

    def out_wait(step, carry):
        peer = z_peer(step)
        out_copy(step, z).wait_send()
        out_copy(step, peer).wait_recv()
        return carry

    lax.fori_loop(1, RING, out_wait, 0)
    mine = pl.ds(pl.multiple_of(x_lo * half_rows, half_rows), half_rows)
    other = pl.ds(pl.multiple_of((1 - x_lo) * half_rows, half_rows), half_rows)
    remote(student_out.at[mine], student_out.at[mine], outx_ss, outx_rs, partner_x).start()
    remote(student_out.at[mine], student_out.at[mine], outx_ss, outx_rs, partner_x).wait_send()
    remote(student_out.at[other], student_out.at[other], outx_ss, outx_rs, partner_x).wait_recv()


def per_device(teacher_features, student_features, prototypes):
    vmem = pltpu.VMEM
    dma = pltpu.SemaphoreType.DMA
    proto_grad, student_grad, loss = pl.pallas_call(
        kernel,
        out_shape=(
            jax.ShapeDtypeStruct((SHARE, COLS), BF16),
            jax.ShapeDtypeStruct((ROWS, WIDTH), BF16),
            jax.ShapeDtypeStruct((1, 128), F32),
        ),
        in_specs=[pl.BlockSpec(memory_space=pl.ANY)] * 3,
        out_specs=(pl.BlockSpec(memory_space=vmem),) * 3,
        scratch_shapes=[
            vmem((ROWS, WIDTH), BF16),
            vmem((ROWS, WIDTH), BF16),
            vmem((WIDTH, COLS), BF16),
            vmem((ROWS, WIDTH), BF16),
            vmem((WIDTH, ROWS), BF16),
            vmem((WIDTH, COLS), BF16),
            vmem((1, COLS), F32),
            vmem((ROWS, COLS), F32),
            vmem((ROWS, COLS), F32),
            vmem((ROWS, COLS), BF16),
            vmem((ROWS, 128), F32),
            vmem((TILES, 128), F32),
            vmem((ITERS, TILES, 128), BF16),
            vmem((ITERS, GRP, TILES, 128), BF16),
            vmem((TILES, 128), F32),
            vmem((ITERS, 8, 128), F32),
            vmem((ITERS, 8, 128), F32),
            vmem((ITERS, RING, 8, 128), F32),
            vmem((ROWS, WIDTH), F32),
            vmem((2, ROWS // 2, WIDTH), BF16),
            vmem((2, ROWS // 2, WIDTH), BF16),
            vmem((2, ROWS // 2, WIDTH), BF16),
            vmem((2, ROWS // 2, WIDTH), F32),
            vmem((2, RING, OWN, WIDTH), BF16),
            vmem((CHIPS, 2, SHARE, BLOCK), F32),
            vmem((BLOCKS, CHIPS, SHARE, BLOCK), BF16),
            vmem((BLOCKS, CHIPS, SHARE, BLOCK), BF16),
            vmem((BLOCKS, CHIPS, SHARE, BLOCK), F32),
            vmem((BLOCKS, CHIPS, SHARE, BLOCK), BF16),
            vmem((BLOCKS, CHIPS, SHARE, BLOCK), BF16),
            vmem((TILES, 128), F32),
            vmem((TILES + 16, 128), BF16),
            vmem((GRP, TILES + 16, 128), BF16),
            dma((3,)),
            dma((ITERS, GRP)),
            dma((ITERS, GRP)),
            dma((ITERS,)),
            dma((ITERS,)),
            dma((ITERS, RING)),
            dma((ITERS, RING)),
            dma((2,)),
            dma((2,)),
            dma((2, RING)),
            dma((2, RING)),
            dma((RING,)),
            dma((RING,)),
            dma,
            dma,
            dma((BLOCKS,)),
            dma((BLOCKS,)),
            dma((BLOCKS, CHIPS)),
            dma((BLOCKS, CHIPS)),
            dma((GRP,)),
            dma((GRP,)),
        ],
        compiler_params=pltpu.CompilerParams(
            collective_id=0, has_side_effects=True, vmem_limit_bytes=56 * 2**20
        ),
        name="sinkhorn_step",
    )(teacher_features, student_features, prototypes)
    return proto_grad, student_grad, loss[0, 0]


def solution(mesh):
    placed = (P("grp", None), P("grp", None), P(None, "proto"))
    return jax.shard_map(
        per_device,
        mesh=mesh,
        in_specs=placed,
        out_specs=(P("grp", "proto"), P("grp", None), P()),
        check_vma=False,
    )
```

time: 795 us -> 107 us (0.13)
  blocking collectives: 572 us -> 0 us
  waiting for transfers between devices: 114 us -> 0 us
  Pallas kernels: 0 us -> 102 us
  matrix products: 61 us -> 0 us
  other arithmetic: 20 us -> 0 us
  between operations: 18 us -> 2.39 us
    psum x8 -> x0, blocking collectives: 572 us -> none  [the longest x3 224 us: column_totals(): return lax.psum(local_mass, 'grp')]
    psum x1 -> x0, waiting for transfers between devices: 114 us -> none  [per_device(): unit_grad = lax.psum(local_unit, 'proto')]
    pallas_call x0 -> x1, Pallas kernels: none -> 102 us  [per_device(): pl.pallas_call(kernel, out_shape=(jax.ShapeDtypeStruct((SHARE, COLS), BF1...]
    dot_general x10 -> x0, matrix products: 61 us -> none  [the longest x3 28.3 us: row_totals(): local_mass = jnp.dot(exps, col_scale, precision=highest)]
    reduce_sum x6 -> x0, other arithmetic: 13.8 us -> none  [the longest x1 8.16 us: per_device(): loss_local = -jnp.sum(targets * log_probs)]
  transfers between devices with their start and end apart: 2 -> 0, of which waited for: 1 -> 0; matrix products, arithmetic and copies ran while one was open for 1% -> 0% of each run, Pallas kernels for 0% -> 0%
where the time goes in v1:
time: 107 us
  Pallas kernels  102 us (95%)
  local copies, waits for them, and re-layouts  3.24 us (3%)
  between operations  2.39 us (2%)
    pallas_call x1, Pallas kernels, per_device(): pl.pallas_call(kernel, out_shape=(jax.ShapeDtypeStruct((SHARE, COLS), BF1...  102 us
    unnamed x2, local copies, waits for them, and re-layouts  3.24 us

profile of v1, /device:TPU:1, one launch (start us, length us, event | category | flops | bytes accessed | tf_op | source)
XLA Modules:
  0.0 107.3 jit_solution(4566635545197872951)
XLA Ops:
  0.6 101.6 %sinkhorn_step.1 = (bf16[16,4096]{1,0:T(8,128)(2,1)}, bf16[512,256]{1,0:T(8,128)(2,1)}, f32[1,128]{1,0:T(1,128)}) custom-call(bf16[512,256]{1,0:T(8,128)(2,1)} %teacher_hbm.1, bf16[512,256]{1,0:T(8,128)(2,1)} %student_hbm.1, bf16[256,4096]{1,0:T(8,128)(2,1)} %proto_hbm.1), custom_call_target="tpu_custom_call" | custom-call | tf_op jit(solution)/shard_map/sinkhorn_step/pallas_call | solution.py:555
  102.3 1.6 %copy.9 = bf16[16,4096]{1,0:T(8,128)(2,1)} copy(bf16[16,4096]{1,0:T(8,128)(2,1)} %get-tuple-element.12) | data formatting | bytes 262144
  103.9 1.7 %copy.10 = bf16[512,256]{1,0:T(8,128)(2,1)} copy(bf16[512,256]{1,0:T(8,128)(2,1)} %get-tuple-element.13) | data formatting | bytes 524288

commit v2 on v1

--- a/solution.py
+++ b/solution.py
@@ -28,6 +28,9 @@
 BLOCK = 512
 BLOCKS = COLS // BLOCK
 TILES = COLS // 128
+TERM_BLOCK = 1024
+TERM_BLOCKS = COLS // TERM_BLOCK
+HALF_ROWS = ROWS // 2
 SHARE = WIDTH // GRP
 CHIPS = 8
 OWN = ROWS // (2 * RING)
@@ -61,10 +64,12 @@
     student_unit,
     student_turned,
     proto_unit,
+    proto_turned,
     proto_scale,
     exps,
     soft,
-    half,
+    soft_half,
+    target_half,
     row_wide,
     col_sums,
     col_send,
@@ -73,6 +78,9 @@
     row_send,
     row_pair,
     row_recv,
+    loss_row,
+    loss_pair,
+    loss_recv,
     unit_part,
     unit_send,
     unit_pair,
@@ -95,6 +103,10 @@
     rowx_rs,
     rowz_ss,
     rowz_rs,
+    lossx_ss,
+    lossx_rs,
+    lossz_ss,
+    lossz_rs,
     unitx_ss,
     unitx_rs,
     unitz_ss,
@@ -128,6 +140,16 @@
     def chip_peer(step):
         return lax.rem(chip + step, CHIPS)
 
+    def each_z(visit):
+        visit(RING // 2)
+
+        def pair(step, carry):
+            visit(RING // 2 - step)
+            visit(RING // 2 + step)
+            return carry
+
+        lax.fori_loop(1, RING // 2, pair, 0)
+
     def remote(src, dst, send, recv, device):
         return pltpu.make_async_remote_copy(
             src_ref=src, dst_ref=dst, send_sem=send, recv_sem=recv, device_id=device, device_id_type=MESH
@@ -150,10 +172,18 @@
     loads = [
         pltpu.make_async_copy(teacher_hbm, teacher_in, in_sem.at[0]),
         pltpu.make_async_copy(student_hbm, student_in, in_sem.at[1]),
-        pltpu.make_async_copy(proto_hbm, proto_in, in_sem.at[2]),
     ]
-    for load in loads:
-        load.start()
+
+    def columns(block, size=BLOCK):
+        return pl.ds(pl.multiple_of(block * size, size), size)
+
+    def proto_load(block):
+        cols = columns(block)
+        return pltpu.make_async_copy(proto_hbm.at[:, cols], proto_in.at[:, cols], in_sem.at[2 + block])
+
+    loads[0].start()
+    lax.fori_loop(0, BLOCKS, lambda block, carry: (proto_load(block).start(), carry)[1], 0)
+    loads[1].start()
 
     def unit_rows(features):
         wide = features.astype(F32)
@@ -161,15 +191,10 @@
         return wide * scaling, scaling
 
     loads[0].wait()
-    loads[1].wait()
     teacher_in[...] = unit_rows(teacher_in[...])[0].astype(BF16)
-    student_unit[...] = unit_rows(student_in[...])[0].astype(BF16)
-    loads[2].wait()
-
-    def columns(block):
-        return pl.ds(pl.multiple_of(block * BLOCK, BLOCK), BLOCK)
 
     def teacher_block(block, carry):
+        proto_load(block).wait()
         cols = columns(block)
         wide = proto_in[:, cols].astype(F32)
         scaling = lax.rsqrt(jnp.sum(wide * wide, axis=0, keepdims=True) + EPSILON)
@@ -213,66 +238,74 @@
             total = total + col_recv[turn, peer].astype(F32)
         col_scale[...] = 1.0 / (ALL_COLS * total)
 
-    def row_start(turn):
-        rows = pl.ds(0, 4 if turn == 1 else 8)
-        copy = remote(
-            row_send.at[turn, rows], row_pair.at[turn, rows], rowx_ss.at[turn], rowx_rs.at[turn], partner_x
-        )
-        copy.start()
-        return copy
-
-    def row_ring(turn, copy):
-        size = 4 if turn == 1 else 8
-        rows = pl.ds(0, size)
-        copy.wait()
-        total = row_send[turn, rows] + row_pair[turn, rows]
-        row_send[turn, rows] = total
-        row_recv[turn, z, rows] = total
-
-        def send(step, carry):
+    def pair_copy(send, pair, send_sem, recv_sem):
+        return remote(send, pair, send_sem, recv_sem, partner_x)
+
+    def ring_start(source, slots, send_sems, recv_sems):
+        def send(step):
             peer = z_peer(step)
             remote(
-                row_send.at[turn, rows],
-                row_recv.at[turn, z, rows],
-                rowz_ss.at[turn, step],
-                rowz_rs.at[turn, z],
-                (grp, x_lo * RING + peer),
+                source, slots.at[z], send_sems.at[step], recv_sems.at[z], (grp, x_lo * RING + peer)
             ).start()
-            return carry
-
-        lax.fori_loop(1, RING, send, 0)
-
-    def row_finish(turn):
-        size = 4 if turn == 1 else 8
-        rows = pl.ds(0, size)
-
+
+        each_z(send)
+
+    def ring_sum(source, slots, send_sems, recv_sems):
         def wait(step, carry):
             peer = z_peer(step)
             remote(
-                row_send.at[turn, rows],
-                row_recv.at[turn, peer, rows],
-                rowz_ss.at[turn, step],
-                rowz_rs.at[turn, peer],
-                (grp, x_lo * RING + peer),
+                source, slots.at[peer], send_sems.at[step], recv_sems.at[peer], (grp, x_lo * RING + peer)
             ).wait()
             return carry
 
         lax.fori_loop(1, RING, wait, 0)
-        total = row_recv[turn, 0, rows]
+        total = slots[0]
         for peer in range(1, RING):
-            total = total + row_recv[turn, peer, rows]
+            total = total + slots[peer]
         return total
 
-    def row_pass(last):
+    def row_refs(turn):
+        rows = pl.ds(0, 8 if turn == 0 else 4)
+        return row_send.at[turn, rows], row_pair.at[turn, rows], row_recv.at[turn, :, rows]
+
+    def row_start(turn):
+        send, pair, slots = row_refs(turn)
+        copy = pair_copy(send, pair, rowx_ss.at[turn], rowx_rs.at[turn])
+        copy.start()
+        return copy
+
+    def row_ring(turn, copy):
+        send, pair, slots = row_refs(turn)
+        copy.wait()
+        total = send[...] + pair[...]
+        send[...] = total
+        slots[z] = total
+        ring_start(send, slots, rowz_ss.at[turn], rowz_rs.at[turn])
+
+    def row_finish(turn):
+        send, pair, slots = row_refs(turn)
+        return ring_sum(send, slots, rowz_ss.at[turn], rowz_rs.at[turn])
+
+    def row_pass():
+        def rows_of(block, carry):
+            rows = pl.ds(pl.multiple_of(block * 64, 64), 64)
+            partial = jnp.zeros((64, 128), F32)
+            for tile in range(TILES):
+                partial = partial + exps[rows, pl.ds(tile * 128, 128)] * col_scale[pl.ds(tile, 1), :]
+            row_wide[rows, :] = partial
+            return carry
+
+        lax.fori_loop(0, ROWS // 64, rows_of, 0)
+        return fold_lanes(row_wide[...])
+
+    def target_pass():
         def rows_of(block, carry):
             rows = pl.ds(pl.multiple_of(block * 64, 64), 64)
             partial = jnp.zeros((64, 128), F32)
             for tile in range(TILES):
                 cols = pl.ds(tile * 128, 128)
                 scaled = exps[rows, cols] * col_scale[pl.ds(tile, 1), :]
-                if last:
-                    exps[rows, cols] = scaled
-                    half[rows, cols] = scaled.astype(BF16)
+                target_half[rows, cols] = scaled.astype(BF16)
                 partial = partial + scaled
             row_wide[rows, :] = partial
             return carry
@@ -295,17 +328,15 @@
 
         lax.fori_loop(0, BLOCKS, block_of, 0)
 
-    def unit_matmul():
-        unit_part[...] = lax.dot_general(
-            half[...], proto_unit[...], (((1,), (1,)), ((), ())), preferred_element_type=F32
-        )
-
-    half_rows = ROWS // 2
+    mine = pl.ds(pl.multiple_of(x_lo * HALF_ROWS, HALF_ROWS), HALF_ROWS)
+    other = pl.ds(pl.multiple_of((1 - x_lo) * HALF_ROWS, HALF_ROWS), HALF_ROWS)
+
+    def unit_matmul(source, rows):
+        unit_part[rows, :] = jnp.dot(source[rows, :], proto_turned[...], preferred_element_type=F32)
 
     def unit_start(part):
-        unit_send[part] = unit_part[pl.ds(pl.multiple_of((1 - x_lo) * half_rows, half_rows), half_rows), :].astype(BF16)
-        unit_mine[part] = unit_part[pl.ds(pl.multiple_of(x_lo * half_rows, half_rows), half_rows), :]
-        copy = remote(unit_send.at[part], unit_pair.at[part], unitx_ss.at[part], unitx_rs.at[part], partner_x)
+        unit_send[part] = unit_part[other, :].astype(BF16)
+        copy = pair_copy(unit_send.at[part], unit_pair.at[part], unitx_ss.at[part], unitx_rs.at[part])
         copy.start()
         return copy
 
@@ -314,11 +345,11 @@
 
     def unit_ring(part, copy):
         copy.wait()
-        total = unit_mine[part] + unit_pair[part].astype(F32)
+        total = unit_part[mine, :] + unit_pair[part].astype(F32)
         unit_mine[part] = total
         unit_share[part] = total.astype(BF16)
 
-        def send(step, carry):
+        def send(step):
             peer = z_peer(step)
             remote(
                 unit_share.at[part, own_rows(peer)],
@@ -327,9 +358,8 @@
                 unitz_rs.at[part, z],
                 (grp, x_lo * RING + peer),
             ).start()
-            return carry
-
-        lax.fori_loop(1, RING, send, 0)
+
+        each_z(send)
 
     def unit_finish(part):
         def wait(step, total):
@@ -346,6 +376,8 @@
         return lax.fori_loop(1, RING, wait, unit_mine[part, own_rows(z), :])
 
     col_start(0)
+    loads[1].wait()
+    student_unit[...] = unit_rows(student_in[...])[0].astype(BF16)
 
     def student_block(block, carry):
         cols = columns(block)
@@ -362,9 +394,17 @@
     lax.fori_loop(0, BLOCKS, student_block, 0)
     row_send[0, 4:8] = fold_lanes(row_wide[...])
     col_finish(0)
-    row_send[0, 0:4] = row_pass(False)
+    row_send[0, 0:4] = row_pass()
     copy = row_start(0)
+    student_turned[...] = student_unit[...].astype(F32).T.astype(BF16)
     row_ring(0, copy)
+
+    def turn_block(block, carry):
+        cols = columns(block)
+        proto_turned[cols, :] = proto_unit[:, cols].T
+        return carry
+
+    lax.fori_loop(0, BLOCKS, turn_block, 0)
     sums = row_finish(0)
     row_scale = 1.0 / (ALL_ROWS * sums[0:4])
     student_total = sums[4:8]
@@ -379,19 +419,16 @@
         scale = row_wide[rows, :]
         for tile in range(TILES):
             cols = pl.ds(tile * 128, 128)
-            scaled = soft[rows, cols] * scale
-            soft[rows, cols] = scaled
-            half[rows, cols] = scaled.astype(BF16)
+            soft_half[rows, cols] = (soft[rows, cols] * scale).astype(BF16)
         return carry
 
     lax.fori_loop(0, ROWS // 64, soft_rows, 0)
-    unit_matmul()
-    unit_copy = unit_start(0)
+    unit_matmul(soft_half, pl.ds(0, ROWS))
     col_finish(1)
-    row_send[1, 0:4] = row_pass(False)
+    row_send[1, 0:4] = row_pass()
     copy = row_start(1)
     row_ring(1, copy)
-    student_turned[...] = student_unit[...].astype(F32).T.astype(BF16)
+    unit_copy = unit_start(0)
     row_scale = 1.0 / (ALL_ROWS * row_finish(1))
 
     row_wide[...] = lane_broadcast(row_scale)
@@ -399,21 +436,25 @@
     col_start(2)
     unit_ring(0, unit_copy)
     col_finish(2)
-    row_send[2, 0:4] = row_pass(True)
-    unit_matmul()
+    row_send[2, 0:4] = target_pass()
+    copy = row_start(2)
+    unit_matmul(target_half, other)
+    unit_copy = unit_start(1)
+    unit_matmul(target_half, mine)
+    row_ring(2, copy)
     row_wide[...] = unit_part[:, :128] * student_unit[:, :128].astype(F32) + unit_part[:, 128:] * student_unit[
         :, 128:
     ].astype(F32)
-    row_send[2, 4:8] = fold_lanes(row_wide[...])
-    copy = row_start(2)
-    unit_copy = unit_start(1)
-    row_ring(2, copy)
+    loss_row[...] = fold_lanes(row_wide[...])
+    loss_copy = pair_copy(loss_row, loss_pair, lossx_ss, lossx_rs)
+    loss_copy.start()
     unit_ring(1, unit_copy)
+    loss_copy.wait()
+    loss_row[...] = loss_row[...] + loss_pair[...]
+    loss_recv[z] = loss_row[...]
+    ring_start(loss_row, loss_recv, lossz_ss, lossz_rs)
     soft_unit = unit_finish(0)
-    sums = row_finish(2)
-    row_scale = 1.0 / (ALL_ROWS * sums[0:4])
-    agreement = (ALL_ROWS / STUDENT_TEMP) * row_scale * sums[4:8]
-    loss_here = jnp.sum(jnp.log(student_total) - agreement) * (1.0 / ALL_ROWS)
+    row_scale = 1.0 / (ALL_ROWS * row_finish(2))
     row_wide[...] = lane_broadcast((ALL_ROWS / STUDENT_TEMP) * row_scale)
 
     def core_copy(block):
@@ -439,19 +480,17 @@
         lax.fori_loop(1, CHIPS, send, 0)
 
     def term_block(block, carry):
-        cols = columns(block)
-        scale = row_wide[...]
-
-        wide_scale = jnp.concatenate([scale] * (BLOCK // 128), axis=1)
-        half[:, cols] = (soft[:, cols] - exps[:, cols] * wide_scale).astype(BF16)
-        product = jnp.dot(student_turned[...], half[:, cols], preferred_element_type=F32)
+        cols = columns(block, TERM_BLOCK)
+        scale = jnp.concatenate([row_wide[...]] * (TERM_BLOCK // 128), axis=1)
+        dlogits = (soft_half[:, cols].astype(F32) - target_half[:, cols].astype(F32) * scale).astype(BF16)
+        product = jnp.dot(student_turned[...], dlogits, preferred_element_type=F32)
+        term[...] = product.reshape(CHIPS, 2, SHARE, TERM_BLOCK)
+        core_send[block] = term[:, 1 - core].astype(BF16)
+        core_copy(block).start()
+        term_mine[block] = term[:, core]
         total = jnp.sum(product * proto_in[:, cols].astype(F32), axis=0, keepdims=True) * proto_scale[:, cols]
-        for tile in range(BLOCK // 128):
-            dots[pl.ds(block * (BLOCK // 128) + tile, 1), :] = total[:, tile * 128 : (tile + 1) * 128]
-        term[...] = product.reshape(CHIPS, 2, SHARE, BLOCK)
-        core_send[block] = term[:, 1 - core].astype(BF16)
-        term_mine[block] = term[:, core]
-        core_copy(block).start()
+        for tile in range(TERM_BLOCK // 128):
+            dots[pl.ds(block * (TERM_BLOCK // 128) + tile, 1), :] = total[:, tile * 128 : (tile + 1) * 128]
 
         @pl.when(block > 0)
         def _():
@@ -459,8 +498,10 @@
 
         return carry
 
-    lax.fori_loop(0, BLOCKS, term_block, 0)
-    term_ring(BLOCKS - 1)
+    lax.fori_loop(0, TERM_BLOCKS, term_block, 0)
+    term_ring(TERM_BLOCKS - 1)
+    agreement = (ALL_ROWS / STUDENT_TEMP) * row_scale * ring_sum(loss_row, loss_recv, lossz_ss, lossz_rs)
+    loss_here = jnp.sum(jnp.log(student_total) - agreement) * (1.0 / ALL_ROWS)
 
     high = loss_here.astype(BF16).astype(F32)
     middle = (loss_here - high).astype(BF16).astype(F32)
@@ -496,7 +537,12 @@
             (grp, x_lo * RING + peer),
         )
 
-    lax.fori_loop(1, RING, lambda step, carry: (out_copy(step, z).start(), carry)[1], 0)
+    def forward(index, owner):
+        rows = own_rows(index * RING + owner)
+        return remote(student_out.at[rows], student_out.at[rows], outx_ss.at[owner], outx_rs.at[owner], partner_x)
+
+    each_z(lambda step: out_copy(step, z).start())
+    forward(x_lo, z).start()
 
     def dot_wait(step, carry):
         peer = grp_peer(step)
@@ -510,8 +556,21 @@
     dots[...] = total[0:TILES]
     loss_out[...] = total[TILES : TILES + 1] + total[TILES + 1 : TILES + 2] + total[TILES + 2 : TILES + 3]
 
+    def pass_on(step):
+        peer = z_peer(step)
+        out_copy(step, peer).wait_recv()
+        forward(x_lo, peer).start()
+
+    def pass_pair(step, carry):
+        pass_on(step)
+        pass_on(RING - step)
+        return carry
+
+    lax.fori_loop(1, RING // 2, pass_pair, 0)
+    pass_on(RING // 2)
+
     def term_finish(block, carry):
-        cols = columns(block)
+        cols = columns(block, TERM_BLOCK)
 
         def wait(step, total):
             peer = chip_peer(step)
@@ -528,25 +587,36 @@
         scaling = proto_scale[:, cols]
         wide = proto_in[pl.ds(pl.multiple_of(grp * SHARE, SHARE), SHARE), cols].astype(F32) * scaling
         dot = jnp.concatenate(
-            [dots[pl.ds(block * (BLOCK // 128) + tile, 1), :] for tile in range(BLOCK // 128)], axis=1
+            [dots[pl.ds(block * (TERM_BLOCK // 128) + tile, 1), :] for tile in range(TERM_BLOCK // 128)], axis=1
         )
         proto_out[:, cols] = ((total - wide * dot) * scaling).astype(BF16)
         return carry
 
-    lax.fori_loop(0, BLOCKS, term_finish, 0)
+    lax.fori_loop(0, TERM_BLOCKS, term_finish, 0)
 
     def out_wait(step, carry):
-        peer = z_peer(step)
         out_copy(step, z).wait_send()
-        out_copy(step, peer).wait_recv()
         return carry
 
     lax.fori_loop(1, RING, out_wait, 0)
-    mine = pl.ds(pl.multiple_of(x_lo * half_rows, half_rows), half_rows)
-    other = pl.ds(pl.multiple_of((1 - x_lo) * half_rows, half_rows), half_rows)
-    remote(student_out.at[mine], student_out.at[mine], outx_ss, outx_rs, partner_x).start()
-    remote(student_out.at[mine], student_out.at[mine], outx_ss, outx_rs, partner_x).wait_send()
-    remote(student_out.at[other], student_out.at[other], outx_ss, outx_rs, partner_x).wait_recv()
+
+    def forward_wait(owner, carry):
+        forward(x_lo, owner).wait_send()
+        forward(1 - x_lo, owner).wait_recv()
+        return carry
+
+    lax.fori_loop(0, RING, forward_wait, 0)
+
+
+def hand_out(proto_in, student_in, proto_out, student_out, sems):
+    copies = [
+        pltpu.make_async_copy(proto_in, proto_out, sems.at[0]),
+        pltpu.make_async_copy(student_in, student_out, sems.at[1]),
+    ]
+    for copy in copies:
+        copy.start()
+    for copy in copies:
+        copy.wait()
 
 
 def per_device(teacher_features, student_features, prototypes):
@@ -568,9 +638,11 @@
             vmem((ROWS, WIDTH), BF16),
             vmem((WIDTH, ROWS), BF16),
             vmem((WIDTH, COLS), BF16),
+            vmem((COLS, WIDTH), BF16),
             vmem((1, COLS), F32),
             vmem((ROWS, COLS), F32),
             vmem((ROWS, COLS), F32),
+            vmem((ROWS, COLS), BF16),
             vmem((ROWS, COLS), BF16),
             vmem((ROWS, 128), F32),
             vmem((TILES, 128), F32),
@@ -580,40 +652,47 @@
             vmem((ITERS, 8, 128), F32),
             vmem((ITERS, 8, 128), F32),
             vmem((ITERS, RING, 8, 128), F32),
+            vmem((4, 128), F32),
+            vmem((4, 128), F32),
+            vmem((RING, 4, 128), F32),
             vmem((ROWS, WIDTH), F32),
             vmem((2, ROWS // 2, WIDTH), BF16),
             vmem((2, ROWS // 2, WIDTH), BF16),
             vmem((2, ROWS // 2, WIDTH), BF16),
             vmem((2, ROWS // 2, WIDTH), F32),
             vmem((2, RING, OWN, WIDTH), BF16),
-            vmem((CHIPS, 2, SHARE, BLOCK), F32),
-            vmem((BLOCKS, CHIPS, SHARE, BLOCK), BF16),
-            vmem((BLOCKS, CHIPS, SHARE, BLOCK), BF16),
-            vmem((BLOCKS, CHIPS, SHARE, BLOCK), F32),
-            vmem((BLOCKS, CHIPS, SHARE, BLOCK), BF16),
-            vmem((BLOCKS, CHIPS, SHARE, BLOCK), BF16),
+            vmem((CHIPS, 2, SHARE, TERM_BLOCK), F32),
+            vmem((TERM_BLOCKS, CHIPS, SHARE, TERM_BLOCK), BF16),
+            vmem((TERM_BLOCKS, CHIPS, SHARE, TERM_BLOCK), BF16),
+            vmem((TERM_BLOCKS, CHIPS, SHARE, TERM_BLOCK), F32),
+            vmem((TERM_BLOCKS, CHIPS, SHARE, TERM_BLOCK), BF16),
+            vmem((TERM_BLOCKS, CHIPS, SHARE, TERM_BLOCK), BF16),
             vmem((TILES, 128), F32),
             vmem((TILES + 16, 128), BF16),
             vmem((GRP, TILES + 16, 128), BF16),
-            dma((3,)),
+            dma((2 + BLOCKS,)),
             dma((ITERS, GRP)),
             dma((ITERS, GRP)),
             dma((ITERS,)),
             dma((ITERS,)),
             dma((ITERS, RING)),
             dma((ITERS, RING)),
+            dma,
+            dma,
+            dma((RING,)),
+            dma((RING,)),
             dma((2,)),
             dma((2,)),
             dma((2, RING)),
             dma((2, RING)),
             dma((RING,)),
             dma((RING,)),
-            dma,
-            dma,
-            dma((BLOCKS,)),
-            dma((BLOCKS,)),
-            dma((BLOCKS, CHIPS)),
-            dma((BLOCKS, CHIPS)),
+            dma((RING,)),
+            dma((RING,)),
+            dma((TERM_BLOCKS,)),
+            dma((TERM_BLOCKS,)),
+            dma((TERM_BLOCKS, CHIPS)),
+            dma((TERM_BLOCKS, CHIPS)),
             dma((GRP,)),
             dma((GRP,)),
         ],
@@ -622,6 +701,17 @@
         ),
         name="sinkhorn_step",
     )(teacher_features, student_features, prototypes)
+    proto_grad, student_grad = pl.pallas_call(
+        hand_out,
+        out_shape=(
+            jax.ShapeDtypeStruct((SHARE, COLS), BF16),
+            jax.ShapeDtypeStruct((ROWS, WIDTH), BF16),
+        ),
+        in_specs=[pl.BlockSpec(memory_space=pltpu.HBM)] * 2,
+        out_specs=(pl.BlockSpec(memory_space=pltpu.HBM),) * 2,
+        scratch_shapes=[dma((2,))],
+        name="hand_out",
+    )(proto_grad, student_grad)
     return proto_grad, student_grad, loss[0, 0]
 
 

time: 107 us -> 110 us (1.028)
  Pallas kernels: 102 us -> 107 us
  local copies, waits for them, and re-layouts: 3.24 us -> 0 us
    pallas_call x0 -> x1, Pallas kernels: none -> 13 us  [per_device(): pl.pallas_call(hand_out, out_shape=(jax.ShapeDtypeStruct((SHARE, COLS), B...]
    pallas_call x1, Pallas kernels: 102 us -> 94.3 us  [per_device(): pl.pallas_call(kernel, out_shape=(jax.ShapeDtypeStruct((SHARE, COLS), BF1...]
    unnamed x2 -> x0, local copies, waits for them, and re-layouts: 3.24 us -> none
where the time goes in v2:
time: 110 us
  Pallas kernels  107 us (97%)
  between operations  2.46 us (2%)
    pallas_call x1, Pallas kernels, per_device(): pl.pallas_call(kernel, out_shape=(jax.ShapeDtypeStruct((SHARE, COLS), BF1...  94.3 us
    pallas_call x1, Pallas kernels, per_device(): pl.pallas_call(hand_out, out_shape=(jax.ShapeDtypeStruct((SHARE, COLS), B...  13 us

profile of v2, /device:TPU:1, one launch (start us, length us, event | category | flops | bytes accessed | tf_op | source)
XLA Modules:
  0.0 109.8 jit_solution(10278320103257026656)
XLA Ops:
  0.6 94.3 %sinkhorn_step.1 = (bf16[16,4096]{1,0:T(8,128)(2,1)}, bf16[512,256]{1,0:T(8,128)(2,1)}, f32[1,128]{1,0:T(1,128)}) custom-call(bf16[512,256]{1,0:T(8,128)(2,1)} %teacher_hbm.1, bf16[512,256]{1,0:T(8,128)(2,1)} %student_hbm.1, bf16[256,4096]{1,0:T(8,128)(2,1)} %proto_hbm.1), custom_call_target="tpu_custom_call" | custom-call | tf_op jit(solution)/shard_map/sinkhorn_step/pallas_call | solution.py:625
  94.9 13.0 %hand_out.1 = (bf16[16,4096]{1,0:T(8,128)(2,1)}, bf16[512,256]{1,0:T(8,128)(2,1)}) custom-call(bf16[16,4096]{1,0:T(8,128)(2,1)} %get-tuple-element.8.proto_in, bf16[512,256]{1,0:T(8,128)(2,1)} %get-tuple-element.9.student_in), custom_call_target="tpu_custom_call" | custom-call | tf_op jit(solution)/shard_map/hand_out/pallas_call | solution.py:704

commit v3 on v2

v3 whole, which is shorter than its diff:
```python
import functools
import math

import jax
import jax.numpy as jnp
from jax import lax
from jax.experimental import pallas as pl
from jax.experimental.pallas import tpu as pltpu
from jax.sharding import PartitionSpec as P

MESH = pl.DeviceIdType.MESH
F32 = jnp.float32
BF16 = jnp.bfloat16

ITERS = 3
TEACHER_TEMP = 0.07
STUDENT_TEMP = 0.1
EPSILON = 1e-06
LOG2E = math.log2(math.e)

ROWS = 512
COLS = 4096
WIDTH = 256
GRP = 16
RING = 16
ALL_ROWS = ROWS * GRP
ALL_COLS = COLS * 2 * RING
BLOCK = 512
BLOCKS = COLS // BLOCK
TILES = COLS // 128
TERM_BLOCK = 1024
TERM_BLOCKS = COLS // TERM_BLOCK
HALF_ROWS = ROWS // 2
NEAR = 5
FAR = RING - 1 - 2 * NEAR
SHARE = WIDTH // GRP
CHIPS = 8
OWN = ROWS // (2 * RING)


def lane_broadcast(vector):
    parts = []
    for group in range(4):
        parts.append(jnp.broadcast_to(vector[group : group + 1, :], (128, 128)).T)
    return jnp.concatenate(parts, axis=0)


def fold_lanes(partial):
    parts = []
    for group in range(4):
        block = partial[group * 128 : (group + 1) * 128, :].T
        parts.append(jnp.sum(block, axis=0, keepdims=True))
    return jnp.concatenate(parts, axis=0)


def kernel(
    teacher_hbm,
    student_hbm,
    proto_hbm,
    proto_out,
    student_out,
    loss_out,
    teacher_in,
    student_in,
    proto_in,
    student_unit,
    student_turned,
    proto_unit,
    proto_turned,
    proto_scale,
    exps,
    soft,
    soft_half,
    target_half,
    row_wide,
    col_sums,
    col_send,
    col_recv,
    col_scale,
    row_send,
    row_pair,
    row_recv,
    row_far,
    loss_row,
    loss_pair,
    loss_recv,
    unit_part,
    unit_send,
    unit_pair,
    unit_share,
    unit_recv,
    term,
    core_send,
    core_recv,
    term_mine,
    term_send,
    term_recv,
    dots,
    dot_send,
    dot_recv,
    in_sem,
    col_sem,
    row_x_sem,
    row_near_sem,
    row_far_sem,
    loss_sem,
    unit_x_sem,
    unit_z_sem,
    out_sem,
    core_sem,
    term_sem,
    dot_sem,
):
    grp = lax.axis_index("grp")
    proto = lax.axis_index("proto")
    core = lax.rem(grp, 2)
    chip = lax.div(grp, 2)
    x_lo = lax.div(proto, RING)
    z = lax.rem(proto, RING)
    partner_core = (grp + 1 - 2 * core, proto)
    partner_x = (grp, z + (1 - x_lo) * RING)
    here = x_lo * RING
    across = RING - here

    def grp_peer(step):
        return lax.rem(grp + step, GRP)

    def z_peer(step):
        return lax.rem(z + step, RING)

    def chip_peer(step):
        return lax.rem(chip + step, CHIPS)

    def near_steps(visit):
        def pair(step, carry):
            visit(NEAR + 1 - step)
            visit(RING - NEAR - 1 + step)
            return carry

        lax.fori_loop(1, NEAR + 1, pair, 0)

    def far_steps(visit):
        visit(RING // 2)

        def pair(step, carry):
            visit(RING // 2 - step)
            visit(RING // 2 + step)
            return carry

        lax.fori_loop(1, FAR // 2 + 1, pair, 0)

    def remote(src, dst, sem, device):
        return pltpu.make_async_remote_copy(
            src_ref=src,
            dst_ref=dst,
            send_sem=sem.at[0],
            recv_sem=sem.at[1],
            device_id=device,
            device_id_type=MESH,
        )

    def landed(ref, sem):
        remote(ref, ref, sem, partner_x).wait_recv()

    def left(ref, sem):
        remote(ref, ref, sem, partner_x).wait_send()

    barrier = pltpu.get_barrier_semaphore()

    def greet_grp(step, carry):
        pl.semaphore_signal(barrier, inc=1, device_id=(grp_peer(step), proto), device_id_type=MESH)
        return carry

    def greet_z(step, carry):
        pl.semaphore_signal(barrier, inc=1, device_id=(grp, here + z_peer(step)), device_id_type=MESH)
        return carry

    lax.fori_loop(1, RING, greet_z, 0)
    lax.fori_loop(1, GRP, greet_grp, 0)
    pl.semaphore_signal(barrier, inc=1, device_id=partner_x, device_id_type=MESH)
    far_steps(
        lambda step: pl.semaphore_signal(
            barrier, inc=1, device_id=(grp, across + z_peer(step)), device_id_type=MESH
        )
    )

    loads = [
        pltpu.make_async_copy(teacher_hbm, teacher_in, in_sem.at[0]),
        pltpu.make_async_copy(student_hbm, student_in, in_sem.at[1]),
    ]

    def columns(block, size=BLOCK):
        return pl.ds(pl.multiple_of(block * size, size), size)

    def proto_load(block):
        cols = columns(block)
        return pltpu.make_async_copy(proto_hbm.at[:, cols], proto_in.at[:, cols], in_sem.at[2 + block])

    loads[0].start()
    lax.fori_loop(0, BLOCKS, lambda block, carry: (proto_load(block).start(), carry)[1], 0)
    loads[1].start()

    def unit_rows(features):
        wide = features.astype(F32)
        scaling = lax.rsqrt(jnp.sum(wide * wide, axis=1, keepdims=True) + EPSILON)
        return wide * scaling, scaling

    loads[0].wait()
    teacher_in[...] = unit_rows(teacher_in[...])[0].astype(BF16)

    def teacher_block(block, carry):
        proto_load(block).wait()
        cols = columns(block)
        wide = proto_in[:, cols].astype(F32)
        scaling = lax.rsqrt(jnp.sum(wide * wide, axis=0, keepdims=True) + EPSILON)
        proto_scale[:, cols] = scaling
        unit = (wide * scaling).astype(BF16)
        proto_unit[:, cols] = unit
        product = jnp.dot(teacher_in[...], unit, preferred_element_type=F32)
        values = jnp.exp2(product * (LOG2E / TEACHER_TEMP))
        exps[:, cols] = values
        total = jnp.sum(values, axis=0, keepdims=True)
        for tile in range(BLOCK // 128):
            col_sums[pl.ds(block * (BLOCK // 128) + tile, 1), :] = total[:, tile * 128 : (tile + 1) * 128]
        return carry

    lax.fori_loop(0, BLOCKS, teacher_block, 0)

    pl.semaphore_wait(barrier, GRP - 1 + RING - 1 + 1 + FAR)

    def col_start(turn):
        message = col_sums[...].astype(BF16)
        col_send[turn] = message
        col_recv[turn, GRP - 1] = message

        def send(step, carry):
            remote(
                col_send.at[turn], col_recv.at[turn, GRP - 1 - step], col_sem.at[turn], (grp_peer(step), proto)
            ).start()
            return carry

        lax.fori_loop(1, GRP, send, 0)

    def col_finish(turn):
        arrivals = col_recv.at[turn, pl.ds(0, GRP - 1)]
        landed(arrivals, col_sem.at[turn])
        total = col_recv[turn, 0].astype(F32)
        for slot in range(1, GRP):
            total = total + col_recv[turn, slot].astype(F32)
        col_scale[...] = 1.0 / (ALL_COLS * total)
        left(arrivals, col_sem.at[turn])

    def ring_order(slots):
        total = slots[lax.rem(RING - 1 - z + RING, RING)]
        for index in range(1, RING):
            total = total + slots[lax.rem(index + RING - 1 - z + RING, RING)]
        return total

    def row_refs(turn):
        rows = pl.ds(0, 8 if turn == 0 else 4)
        return (
            row_send.at[turn, rows],
            row_pair.at[turn, 0, rows],
            row_pair.at[turn, 1, rows],
            row_recv.at[turn, :, rows],
            row_far.at[turn, :, rows],
        )

    def row_start(turn):
        send, pair, both, slots, far = row_refs(turn)

        def to_far(step):
            slot = RING // 2 + FAR // 2 - step
            remote(send, far.at[slot], row_far_sem.at[turn], (grp, here + z_peer(step))).start()
            remote(send, far.at[FAR + slot], row_far_sem.at[turn], (grp, across + z_peer(step))).start()

        remote(send, pair, row_x_sem.at[turn], partner_x).start()
        far_steps(to_far)

    def row_ring(turn):
        send, pair, both, slots, far = row_refs(turn)
        landed(pair, row_x_sem.at[turn])
        total = send[...] + pair[...]
        both[...] = total
        slots[RING - 1] = total
        near_steps(
            lambda step: remote(
                both, slots.at[RING - 1 - step], row_near_sem.at[turn], (grp, here + z_peer(step))
            ).start()
        )

    def row_finish(turn):
        send, pair, both, slots, far = row_refs(turn)
        landed(slots.at[pl.ds(0, 2 * NEAR)], row_near_sem.at[turn])
        landed(far, row_far_sem.at[turn])
        for index in range(FAR):
            slots[NEAR + index] = far[index] + far[FAR + index]
        left(pair, row_x_sem.at[turn])
        left(slots.at[pl.ds(0, 2 * NEAR)], row_near_sem.at[turn])
        left(far, row_far_sem.at[turn])
        return ring_order(slots)

    def row_pass():
        def rows_of(block, carry):
            rows = pl.ds(pl.multiple_of(block * 64, 64), 64)
            partial = jnp.zeros((64, 128), F32)
            for tile in range(TILES):
                partial = partial + exps[rows, pl.ds(tile * 128, 128)] * col_scale[pl.ds(tile, 1), :]
            row_wide[rows, :] = partial
            return carry

        lax.fori_loop(0, ROWS // 64, rows_of, 0)
        return fold_lanes(row_wide[...])

    def target_pass():
        def rows_of(block, carry):
            rows = pl.ds(pl.multiple_of(block * 64, 64), 64)
            partial = jnp.zeros((64, 128), F32)
            for tile in range(TILES):
                cols = pl.ds(tile * 128, 128)
                scaled = exps[rows, cols] * col_scale[pl.ds(tile, 1), :]
                target_half[rows, cols] = scaled.astype(BF16)
                partial = partial + scaled
            row_wide[rows, :] = partial
            return carry

        lax.fori_loop(0, ROWS // 64, rows_of, 0)
        return fold_lanes(row_wide[...])

    def col_pass():
        def block_of(block, carry):
            cols = columns(block)
            partial = jnp.zeros((8, BLOCK), F32)
            for group in range(ROWS // 8):
                rows = pl.ds(group * 8, 8)
                scale = row_wide[rows, :]
                partial = partial + exps[rows, cols] * jnp.concatenate([scale] * (BLOCK // 128), axis=1)
            total = jnp.sum(partial, axis=0, keepdims=True)
            for tile in range(BLOCK // 128):
                col_sums[pl.ds(block * (BLOCK // 128) + tile, 1), :] = total[:, tile * 128 : (tile + 1) * 128]
            return carry

        lax.fori_loop(0, BLOCKS, block_of, 0)

    mine = pl.ds(pl.multiple_of(x_lo * HALF_ROWS, HALF_ROWS), HALF_ROWS)
    other = pl.ds(pl.multiple_of((1 - x_lo) * HALF_ROWS, HALF_ROWS), HALF_ROWS)

    def unit_matmul(source, rows):
        unit_part[rows, :] = jnp.dot(source[rows, :], proto_turned[...], preferred_element_type=F32)

    def own_rows(index):
        return pl.ds(pl.multiple_of(index * OWN, OWN), OWN)

    near_rows = pl.ds(0, (2 * NEAR + 1) * OWN)

    def unit_x(part):
        unit_send[part] = unit_part[...].astype(BF16)

        def send(step, carry):
            rows = own_rows(lax.rem(z + step + RING - NEAR, RING))
            theirs = own_rows(across + lax.rem(z + step + RING - NEAR, RING))
            remote(unit_send.at[part, theirs], unit_pair.at[part, rows], unit_x_sem.at[part], partner_x).start()
            return carry

        lax.fori_loop(0, 2 * NEAR + 1, send, 0)

    def unit_far(part):
        def to_far(step):
            peer = z_peer(step)
            slot = 2 * NEAR + RING // 2 + FAR // 2 - step
            remote(
                unit_send.at[part, own_rows(across + peer)],
                unit_recv.at[part, FAR + slot],
                unit_z_sem.at[part],
                (grp, across + peer),
            ).start()
            remote(
                unit_send.at[part, own_rows(here + peer)],
                unit_recv.at[part, slot],
                unit_z_sem.at[part],
                (grp, here + peer),
            ).start()

        far_steps(to_far)

    def unit_near(part):
        landed(unit_pair.at[part, near_rows], unit_x_sem.at[part])

        def to_near(step):
            peer = z_peer(step)
            rows = own_rows(peer)
            total = unit_part[own_rows(here + peer), :] + unit_pair[part, rows, :].astype(F32)
            unit_share[part, rows, :] = total.astype(BF16)
            slot = step - 1 - NEAR * lax.div(step, RING // 2)
            remote(
                unit_share.at[part, rows], unit_recv.at[part, slot], unit_z_sem.at[part], (grp, here + peer)
            ).start()

        near_steps(to_near)

    def unit_own(part):
        return unit_part[own_rows(here + z), :] + unit_pair[part, own_rows(z), :].astype(F32)

    def unit_finish(part, total):
        landed(unit_recv.at[part], unit_z_sem.at[part])
        for slot in range(2 * NEAR + 2 * FAR):
            total = total + unit_recv[part, slot].astype(F32)
        left(unit_pair.at[part, near_rows], unit_x_sem.at[part])
        left(unit_recv.at[part], unit_z_sem.at[part])
        return total

    col_start(0)
    loads[1].wait()
    student_unit[...] = unit_rows(student_in[...])[0].astype(BF16)

    def student_block(block, carry):
        cols = columns(block)
        product = jnp.dot(student_unit[...], proto_unit[:, cols], preferred_element_type=F32)
        values = jnp.exp2(product * (LOG2E / STUDENT_TEMP))
        soft[:, cols] = values
        partial = values[:, :128]
        for tile in range(1, BLOCK // 128):
            partial = partial + values[:, tile * 128 : (tile + 1) * 128]
        row_wide[...] = row_wide[...] + partial
        return carry

    row_wide[...] = jnp.zeros((ROWS, 128), F32)
    lax.fori_loop(0, BLOCKS, student_block, 0)
    row_send[0, 4:8] = fold_lanes(row_wide[...])
    col_finish(0)
    row_send[0, 0:4] = row_pass()
    row_start(0)
    student_turned[...] = student_unit[...].astype(F32).T.astype(BF16)
    row_ring(0)

    def turn_block(block, carry):
        cols = columns(block)
        proto_turned[cols, :] = proto_unit[:, cols].T
        return carry

    lax.fori_loop(0, BLOCKS, turn_block, 0)
    sums = row_finish(0)
    row_scale = 1.0 / (ALL_ROWS * sums[0:4])
    student_total = sums[4:8]

    row_wide[...] = lane_broadcast(row_scale)
    col_pass()
    col_start(1)
    row_wide[...] = lane_broadcast((1.0 / STUDENT_TEMP) / student_total)

    def soft_rows(block, carry):
        rows = pl.ds(pl.multiple_of(block * 64, 64), 64)
        scale = row_wide[rows, :]
        for tile in range(TILES):
            cols = pl.ds(tile * 128, 128)
            soft_half[rows, cols] = (soft[rows, cols] * scale).astype(BF16)
        return carry

    lax.fori_loop(0, ROWS // 64, soft_rows, 0)
    unit_matmul(soft_half, pl.ds(0, ROWS))
    col_finish(1)
    row_send[1, 0:4] = row_pass()
    row_start(1)
    row_ring(1)
    unit_x(0)
    row_scale = 1.0 / (ALL_ROWS * row_finish(1))

    row_wide[...] = lane_broadcast(row_scale)
    col_pass()
    col_start(2)
    unit_far(0)
    unit_near(0)
    soft_own = unit_own(0)
    col_finish(2)
    row_send[2, 0:4] = target_pass()
    row_start(2)
    unit_matmul(target_half, pl.ds(0, ROWS))
    unit_x(1)
    unit_far(1)
    row_ring(2)
    row_wide[...] = unit_part[:, :128] * student_unit[:, :128].astype(F32) + unit_part[:, 128:] * student_unit[
        :, 128:
    ].astype(F32)
    loss_row[0] = fold_lanes(row_wide[...])
    remote(loss_row.at[0], loss_pair, loss_sem.at[0], partner_x).start()
    unit_near(1)
    target_own = unit_own(1)
    landed(loss_pair, loss_sem.at[0])
    loss_row[1] = loss_row[0] + loss_pair[...]
    loss_recv[RING - 1] = loss_row[1]

    def loss_send(step, carry):
        remote(
            loss_row.at[1], loss_recv.at[RING - 1 - step], loss_sem.at[1], (grp, here + z_peer(step))
        ).start()
        return carry

    lax.fori_loop(1, RING, loss_send, 0)
    soft_unit = unit_finish(0, soft_own)
    row_scale = 1.0 / (ALL_ROWS * row_finish(2))
    row_wide[...] = lane_broadcast((ALL_ROWS / STUDENT_TEMP) * row_scale)

    def core_copy(block):
        return remote(core_send.at[block], core_recv.at[block], core_sem.at[block], partner_core)

    def term_ring(block):
        core_copy(block).wait()
        total = term_mine[block] + core_recv[block].astype(F32)
        term_mine[block] = total
        term_send[block] = total.astype(BF16)

        def send(step, carry):
            peer = chip_peer(step)
            remote(
                term_send.at[block, peer],
                term_recv.at[block, CHIPS - 1 - step],
                term_sem.at[block],
                (peer * 2 + core, proto),
            ).start()
            return carry

        lax.fori_loop(1, CHIPS, send, 0)

    def term_block(block, carry):
        cols = columns(block, TERM_BLOCK)
        scale = jnp.concatenate([row_wide[...]] * (TERM_BLOCK // 128), axis=1)
        dlogits = (soft_half[:, cols].astype(F32) - target_half[:, cols].astype(F32) * scale).astype(BF16)
        product = jnp.dot(student_turned[...], dlogits, preferred_element_type=F32)
        term[...] = product.reshape(CHIPS, 2, SHARE, TERM_BLOCK)
        core_send[block] = term[:, 1 - core].astype(BF16)
        core_copy(block).start()
        term_mine[block] = term[:, core]
        total = jnp.sum(product * proto_in[:, cols].astype(F32), axis=0, keepdims=True) * proto_scale[:, cols]
        for tile in range(TERM_BLOCK // 128):
            dots[pl.ds(block * (TERM_BLOCK // 128) + tile, 1), :] = total[:, tile * 128 : (tile + 1) * 128]

        @pl.when(block > 0)
        def _():
            term_ring(block - 1)

        return carry

    lax.fori_loop(0, TERM_BLOCKS, term_block, 0)
    term_ring(TERM_BLOCKS - 1)
    landed(loss_recv.at[pl.ds(0, RING - 1)], loss_sem.at[1])
    agreement = (ALL_ROWS / STUDENT_TEMP) * row_scale * ring_order(loss_recv)
    left(loss_pair, loss_sem.at[0])
    left(loss_recv.at[pl.ds(0, RING - 1)], loss_sem.at[1])
    loss_here = jnp.sum(jnp.log(student_total) - agreement) * (1.0 / ALL_ROWS)

    high = loss_here.astype(BF16).astype(F32)
    middle = (loss_here - high).astype(BF16).astype(F32)
    low = loss_here - high - middle
    place = lax.broadcasted_iota(jnp.int32, (16, 128), 0)
    pieces = jnp.where(place == 0, high, jnp.where(place == 1, middle, jnp.where(place == 2, low, 0.0)))
    dot_send[0:TILES] = dots[...].astype(BF16)
    dot_send[TILES : TILES + 16] = pieces.astype(BF16)
    dot_recv[GRP - 1] = dot_send[...]

    def dot_start(step, carry):
        remote(dot_send, dot_recv.at[GRP - 1 - step], dot_sem, (grp_peer(step), proto)).start()
        return carry

    lax.fori_loop(1, GRP, dot_start, 0)

    target_unit = unit_finish(1, target_own)
    my_rows = own_rows(here + z)
    unit_grad = soft_unit - target_unit * row_wide[my_rows, 0:1]
    wide, scaling = unit_rows(student_in[my_rows, :])
    row_dots = jnp.sum(wide * unit_grad, axis=1, keepdims=True)
    student_out[my_rows, :] = ((unit_grad - wide * row_dots) * scaling).astype(BF16)

    def out_send(step, base, sem):
        rows = student_out.at[my_rows]
        remote(rows, rows, sem, (grp, base + z_peer(step))).start()

    def out_far(step):
        out_send(step, across, out_sem.at[1])
        out_send(step, here, out_sem.at[1])

    def forward(owner):
        rows = student_out.at[own_rows(here + owner)]
        remote(rows, rows, out_sem.at[2], partner_x).start()

    far_steps(out_far)
    near_steps(lambda step: out_send(step, here, out_sem.at[0]))
    forward(z)

    dot_arrivals = dot_recv.at[pl.ds(0, GRP - 1)]
    landed(dot_arrivals, dot_sem)
    total = jnp.zeros((TILES + 16, 128), F32)
    for index in range(GRP):
        total = total + dot_recv[lax.rem(index + GRP - 1 - grp + GRP, GRP)].astype(F32)
    dots[...] = total[0:TILES]
    loss_out[...] = total[TILES : TILES + 1] + total[TILES + 1 : TILES + 2] + total[TILES + 2 : TILES + 3]
    left(dot_arrivals, dot_sem)

    near_out = student_out.at[pl.ds(0, 2 * NEAR * OWN)]
    landed(near_out, out_sem.at[0])
    near_steps(lambda step: forward(z_peer(step)))

    def term_finish(block, carry):
        cols = columns(block, TERM_BLOCK)

        arrivals = term_recv.at[block]
        landed(arrivals, term_sem.at[block])
        total = term_mine[block, chip]
        for slot in range(CHIPS - 1):
            total = total + term_recv[block, slot].astype(F32)
        left(arrivals, term_sem.at[block])
        scaling = proto_scale[:, cols]
        wide = proto_in[pl.ds(pl.multiple_of(grp * SHARE, SHARE), SHARE), cols].astype(F32) * scaling
        dot = jnp.concatenate(
            [dots[pl.ds(block * (TERM_BLOCK // 128) + tile, 1), :] for tile in range(TERM_BLOCK // 128)], axis=1
        )
        proto_out[:, cols] = ((total - wide * dot) * scaling).astype(BF16)
        return carry

    lax.fori_loop(0, TERM_BLOCKS, term_finish, 0)

    far_out = student_out.at[pl.ds(0, 2 * FAR * OWN)]
    passed_out = student_out.at[pl.ds(0, (2 * NEAR + 1) * OWN)]
    landed(far_out, out_sem.at[1])
    landed(passed_out, out_sem.at[2])
    left(near_out, out_sem.at[0])
    left(far_out, out_sem.at[1])
    left(passed_out, out_sem.at[2])


def per_device(teacher_features, student_features, prototypes):
    vmem = pltpu.VMEM
    dma = pltpu.SemaphoreType.DMA
    proto_grad, student_grad, loss = pl.pallas_call(
        kernel,
        out_shape=(
            vmem((SHARE, COLS), BF16),
            vmem((ROWS, WIDTH), BF16),
            jax.ShapeDtypeStruct((1, 128), F32),
        ),
        in_specs=[pl.BlockSpec(memory_space=pl.ANY)] * 3,
        out_specs=(pl.BlockSpec(memory_space=vmem),) * 3,
        scratch_shapes=[
            vmem((ROWS, WIDTH), BF16),
            vmem((ROWS, WIDTH), BF16),
            vmem((WIDTH, COLS), BF16),
            vmem((ROWS, WIDTH), BF16),
            vmem((WIDTH, ROWS), BF16),
            vmem((WIDTH, COLS), BF16),
            vmem((COLS, WIDTH), BF16),
            vmem((1, COLS), F32),
            vmem((ROWS, COLS), F32),
            vmem((ROWS, COLS), F32),
            vmem((ROWS, COLS), BF16),
            vmem((ROWS, COLS), BF16),
            vmem((ROWS, 128), F32),
            vmem((TILES, 128), F32),
            vmem((ITERS, TILES, 128), BF16),
            vmem((ITERS, GRP, TILES, 128), BF16),
            vmem((TILES, 128), F32),
            vmem((ITERS, 8, 128), F32),
            vmem((ITERS, 2, 8, 128), F32),
            vmem((ITERS, RING, 8, 128), F32),
            vmem((ITERS, 2 * FAR, 8, 128), F32),
            vmem((2, 4, 128), F32),
            vmem((4, 128), F32),
            vmem((RING, 4, 128), F32),
            vmem((ROWS, WIDTH), F32),
            vmem((2, ROWS, WIDTH), BF16),
            vmem((2, HALF_ROWS, WIDTH), BF16),
            vmem((2, HALF_ROWS, WIDTH), BF16),
            vmem((2, 2 * NEAR + 2 * FAR, OWN, WIDTH), BF16),
            vmem((CHIPS, 2, SHARE, TERM_BLOCK), F32),
            vmem((TERM_BLOCKS, CHIPS, SHARE, TERM_BLOCK), BF16),
            vmem((TERM_BLOCKS, CHIPS, SHARE, TERM_BLOCK), BF16),
            vmem((TERM_BLOCKS, CHIPS, SHARE, TERM_BLOCK), F32),
            vmem((TERM_BLOCKS, CHIPS, SHARE, TERM_BLOCK), BF16),
            vmem((TERM_BLOCKS, CHIPS - 1, SHARE, TERM_BLOCK), BF16),
            vmem((TILES, 128), F32),
            vmem((TILES + 16, 128), BF16),
            vmem((GRP, TILES + 16, 128), BF16),
            dma((2 + BLOCKS,)),
            dma((ITERS, 2)),
            dma((ITERS, 2)),
            dma((ITERS, 2)),
            dma((ITERS, 2)),
            dma((2, 2)),
            dma((2, 2)),
            dma((2, 2)),
            dma((3, 2)),
            dma((TERM_BLOCKS, 2)),
            dma((TERM_BLOCKS, 2)),
            dma((2,)),
        ],
        compiler_params=pltpu.CompilerParams(
            collective_id=0, has_side_effects=True, vmem_limit_bytes=56 * 2**20
        ),
        name="sinkhorn_step",
    )(teacher_features, student_features, prototypes)
    return proto_grad, student_grad, loss[0, 0]


def solution(mesh):
    placed = (P("grp", None), P("grp", None), P(None, "proto"))
    return jax.shard_map(
        per_device,
        mesh=mesh,
        in_specs=placed,
        out_specs=(P("grp", "proto"), P("grp", None), P()),
        check_vma=False,
    )
```

time: 110 us -> 97.7 us (0.89)
  Pallas kernels: 107 us -> 93.6 us
  local copies, waits for them, and re-layouts: 0 us -> 1.36 us
    pallas_call x2 -> x1, Pallas kernels: 107 us -> 93.6 us  [per_device(): pl.pallas_call(kernel, out_shape=(vmem((SHARE, COLS), BF16), vmem((ROWS,...]
    unnamed x0 -> x2, local copies, waits for them, and re-layouts: none -> 1.36 us
where the time goes in v3:
time: 97.7 us; the launch traced here: 97.3 us
  Pallas kernels  93.6 us (96%)
  between operations  2.33 us (2%)
  local copies, waits for them, and re-layouts  1.36 us (1%)
    pallas_call x1, Pallas kernels, per_device(): pl.pallas_call(kernel, out_shape=(vmem((SHARE, COLS), BF16), vmem((ROWS,...  93.6 us

profile of v3, /device:TPU:1, one launch (start us, length us, event | category | flops | bytes accessed | tf_op | source)
XLA Modules:
  0.0 97.3 jit_solution(798950919476540683)
XLA Ops:
  0.6 93.6 %sinkhorn_step.1 = (bf16[16,4096]{1,0:T(8,128)(2,1)S(1)}, bf16[512,256]{1,0:T(8,128)(2,1)S(1)}, f32[1,128]{1,0:T(1,128)}) custom-call(bf16[512,256]{1,0:T(8,128)(2,1)} %teacher_hbm.1, bf16[512,256]{1,0:T(8,128)(2,1)} %student_hbm.1, bf16[256,4096]{1,0:T(8,128)(2,1)} %proto_hbm.1), custom_call_target="tpu_custom_call" | custom-call | tf_op jit(solution)/shard_map/sinkhorn_step/pallas_call | solution.py:633
  94.2 0.7 copy.9
  94.9 0.7 copy.10

commit v4 on v3

--- a/solution.py
+++ b/solution.py
@@ -28,7 +28,7 @@
 BLOCK = 512
 BLOCKS = COLS // BLOCK
 TILES = COLS // 128
-TERM_BLOCK = 1024
+TERM_BLOCK = 512
 TERM_BLOCKS = COLS // TERM_BLOCK
 HALF_ROWS = ROWS // 2
 NEAR = 5
@@ -78,12 +78,12 @@
     col_recv,
     col_scale,
     row_send,
-    row_pair,
     row_recv,
-    row_far,
     loss_row,
     loss_pair,
     loss_recv,
+    loss_send,
+    loss_all,
     unit_part,
     unit_send,
     unit_pair,
@@ -100,9 +100,7 @@
     dot_recv,
     in_sem,
     col_sem,
-    row_x_sem,
-    row_near_sem,
-    row_far_sem,
+    row_sem,
     loss_sem,
     unit_x_sem,
     unit_z_sem,
@@ -165,25 +163,6 @@
     def left(ref, sem):
         remote(ref, ref, sem, partner_x).wait_send()
 
-    barrier = pltpu.get_barrier_semaphore()
-
-    def greet_grp(step, carry):
-        pl.semaphore_signal(barrier, inc=1, device_id=(grp_peer(step), proto), device_id_type=MESH)
-        return carry
-
-    def greet_z(step, carry):
-        pl.semaphore_signal(barrier, inc=1, device_id=(grp, here + z_peer(step)), device_id_type=MESH)
-        return carry
-
-    lax.fori_loop(1, RING, greet_z, 0)
-    lax.fori_loop(1, GRP, greet_grp, 0)
-    pl.semaphore_signal(barrier, inc=1, device_id=partner_x, device_id_type=MESH)
-    far_steps(
-        lambda step: pl.semaphore_signal(
-            barrier, inc=1, device_id=(grp, across + z_peer(step)), device_id_type=MESH
-        )
-    )
-
     loads = [
         pltpu.make_async_copy(teacher_hbm, teacher_in, in_sem.at[0]),
         pltpu.make_async_copy(student_hbm, student_in, in_sem.at[1]),
@@ -199,6 +178,19 @@
     loads[0].start()
     lax.fori_loop(0, BLOCKS, lambda block, carry: (proto_load(block).start(), carry)[1], 0)
     loads[1].start()
+
+    barrier = pltpu.get_barrier_semaphore()
+
+    def greet_grp(step, carry):
+        pl.semaphore_signal(barrier, inc=1, device_id=(grp_peer(step), proto), device_id_type=MESH)
+        return carry
+
+    def greet_proto(step, carry):
+        pl.semaphore_signal(barrier, inc=1, device_id=(grp, lax.rem(proto + step, 2 * RING)), device_id_type=MESH)
+        return carry
+
+    lax.fori_loop(1, 2 * RING, greet_proto, 0)
+    lax.fori_loop(1, GRP, greet_grp, 0)
 
     def unit_rows(features):
         wide = features.astype(F32)
@@ -226,7 +218,7 @@
 
     lax.fori_loop(0, BLOCKS, teacher_block, 0)
 
-    pl.semaphore_wait(barrier, GRP - 1 + RING - 1 + 1 + FAR)
+    pl.semaphore_wait(barrier, GRP - 1 + 2 * RING - 1)
 
     def col_start(turn):
         message = col_sums[...].astype(BF16)
@@ -250,55 +242,48 @@
         col_scale[...] = 1.0 / (ALL_COLS * total)
         left(arrivals, col_sem.at[turn])
 
+    PEERS = 2 * RING - 1
+
     def ring_order(slots):
         total = slots[lax.rem(RING - 1 - z + RING, RING)]
         for index in range(1, RING):
             total = total + slots[lax.rem(index + RING - 1 - z + RING, RING)]
         return total
 
-    def row_refs(turn):
-        rows = pl.ds(0, 8 if turn == 0 else 4)
-        return (
-            row_send.at[turn, rows],
-            row_pair.at[turn, 0, rows],
-            row_pair.at[turn, 1, rows],
-            row_recv.at[turn, :, rows],
-            row_far.at[turn, :, rows],
-        )
-
-    def row_start(turn):
-        send, pair, both, slots, far = row_refs(turn)
-
-        def to_far(step):
-            slot = RING // 2 + FAR // 2 - step
-            remote(send, far.at[slot], row_far_sem.at[turn], (grp, here + z_peer(step))).start()
-            remote(send, far.at[FAR + slot], row_far_sem.at[turn], (grp, across + z_peer(step))).start()
-
-        remote(send, pair, row_x_sem.at[turn], partner_x).start()
-        far_steps(to_far)
-
-    def row_ring(turn):
-        send, pair, both, slots, far = row_refs(turn)
-        landed(pair, row_x_sem.at[turn])
-        total = send[...] + pair[...]
-        both[...] = total
-        slots[RING - 1] = total
-        near_steps(
-            lambda step: remote(
-                both, slots.at[RING - 1 - step], row_near_sem.at[turn], (grp, here + z_peer(step))
+    def row_start(turn, sums):
+        row_send[turn] = sums
+        row_recv[turn, PEERS] = sums
+
+        def send(step, base, offset):
+            remote(
+                row_send.at[turn],
+                row_recv.at[turn, PEERS - offset - step],
+                row_sem.at[turn],
+                (grp, base + z_peer(step)),
             ).start()
-        )
+
+        def four(step, carry):
+            for base, offset in ((here, 0), (across, RING)):
+                send(RING // 2 - step, base, offset)
+                send(RING // 2 + step, base, offset)
+            return carry
+
+        send(RING // 2, across, RING)
+        send(RING // 2, here, 0)
+        lax.fori_loop(1, RING // 2, four, 0)
+        send(0, across, RING)
 
     def row_finish(turn):
-        send, pair, both, slots, far = row_refs(turn)
-        landed(slots.at[pl.ds(0, 2 * NEAR)], row_near_sem.at[turn])
-        landed(far, row_far_sem.at[turn])
-        for index in range(FAR):
-            slots[NEAR + index] = far[index] + far[FAR + index]
-        left(pair, row_x_sem.at[turn])
-        left(slots.at[pl.ds(0, 2 * NEAR)], row_near_sem.at[turn])
-        left(far, row_far_sem.at[turn])
-        return ring_order(slots)
+        arrivals = row_recv.at[turn, pl.ds(0, PEERS)]
+        landed(arrivals, row_sem.at[turn])
+        total = None
+        for index in range(RING):
+            slot = lax.rem(index + RING - 1 - z + RING, RING)
+            own = row_recv[turn, RING + slot]
+            other = row_recv[turn, slot]
+            total = own + other if total is None else total + (own + other)
+        left(arrivals, row_sem.at[turn])
+        return total
 
     def row_pass():
         def rows_of(block, carry):
@@ -351,62 +336,82 @@
     def own_rows(index):
         return pl.ds(pl.multiple_of(index * OWN, OWN), OWN)
 
+    ring_rows = pl.ds(0, (RING - 1) * OWN)
     near_rows = pl.ds(0, (2 * NEAR + 1) * OWN)
 
-    def unit_x(part):
-        unit_send[part] = unit_part[...].astype(BF16)
+    def soft_x():
+        unit_send[0, other, :] = unit_part[other, :].astype(BF16)
+        remote(unit_send.at[0, other], unit_pair.at[0], unit_x_sem.at[0], partner_x).start()
+
+    def soft_ring():
+        landed(unit_pair.at[0], unit_x_sem.at[0])
+        total = unit_part[mine, :] + unit_pair[0].astype(F32)
+        unit_share[0] = total.astype(BF16)
 
         def send(step, carry):
-            rows = own_rows(lax.rem(z + step + RING - NEAR, RING))
-            theirs = own_rows(across + lax.rem(z + step + RING - NEAR, RING))
-            remote(unit_send.at[part, theirs], unit_pair.at[part, rows], unit_x_sem.at[part], partner_x).start()
+            peer = z_peer(step)
+            remote(
+                unit_share.at[0, own_rows(peer)], unit_recv.at[0, step - 1], unit_z_sem.at[0], (grp, here + peer)
+            ).start()
+            return carry
+
+        lax.fori_loop(1, RING, send, 0)
+
+    def soft_finish(total):
+        landed(unit_recv.at[0, pl.ds(0, RING - 1)], unit_z_sem.at[0])
+        for slot in range(RING - 1):
+            total = total + unit_recv[0, slot].astype(F32)
+        left(unit_pair.at[0], unit_x_sem.at[0])
+        left(unit_share.at[0, ring_rows], unit_z_sem.at[0])
+        return total
+
+    def unit_x():
+        unit_send[1, other, :] = unit_part[other, :].astype(BF16)
+
+        def send(step, carry):
+            owner = lax.rem(z + step + RING - NEAR, RING)
+            remote(
+                unit_send.at[1, own_rows(across + owner)],
+                unit_pair.at[1, own_rows(owner)],
+                unit_x_sem.at[1],
+                partner_x,
+            ).start()
             return carry
 
         lax.fori_loop(0, 2 * NEAR + 1, send, 0)
 
-    def unit_far(part):
+    def unit_far(base, offset):
         def to_far(step):
             peer = z_peer(step)
-            slot = 2 * NEAR + RING // 2 + FAR // 2 - step
+            slot = offset + 2 * NEAR + RING // 2 + FAR // 2 - step
             remote(
-                unit_send.at[part, own_rows(across + peer)],
-                unit_recv.at[part, FAR + slot],
-                unit_z_sem.at[part],
-                (grp, across + peer),
+                unit_send.at[1, own_rows(base + peer)], unit_recv.at[1, slot], unit_z_sem.at[1], (grp, base + peer)
             ).start()
-            remote(
-                unit_send.at[part, own_rows(here + peer)],
-                unit_recv.at[part, slot],
-                unit_z_sem.at[part],
-                (grp, here + peer),
-            ).start()
 
         far_steps(to_far)
 
-    def unit_near(part):
-        landed(unit_pair.at[part, near_rows], unit_x_sem.at[part])
+    def unit_near():
+        landed(unit_pair.at[1, near_rows], unit_x_sem.at[1])
 
         def to_near(step):
             peer = z_peer(step)
             rows = own_rows(peer)
-            total = unit_part[own_rows(here + peer), :] + unit_pair[part, rows, :].astype(F32)
-            unit_share[part, rows, :] = total.astype(BF16)
+            total = unit_part[own_rows(here + peer), :] + unit_pair[1, rows, :].astype(F32)
+            unit_share[1, rows, :] = total.astype(BF16)
             slot = step - 1 - NEAR * lax.div(step, RING // 2)
-            remote(
-                unit_share.at[part, rows], unit_recv.at[part, slot], unit_z_sem.at[part], (grp, here + peer)
-            ).start()
+            remote(unit_share.at[1, rows], unit_recv.at[1, slot], unit_z_sem.at[1], (grp, here + peer)).start()
 
         near_steps(to_near)
 
     def unit_own(part):
         return unit_part[own_rows(here + z), :] + unit_pair[part, own_rows(z), :].astype(F32)
 
-    def unit_finish(part, total):
-        landed(unit_recv.at[part], unit_z_sem.at[part])
+    def unit_finish(total):
+        landed(unit_recv.at[1], unit_z_sem.at[1])
         for slot in range(2 * NEAR + 2 * FAR):
-            total = total + unit_recv[part, slot].astype(F32)
-        left(unit_pair.at[part, near_rows], unit_x_sem.at[part])
-        left(unit_recv.at[part], unit_z_sem.at[part])
+            total = total + unit_recv[1, slot].astype(F32)
+        left(unit_pair.at[1, near_rows], unit_x_sem.at[1])
+        left(unit_recv.at[1], unit_z_sem.at[1])
         return total
 
     col_start(0)
@@ -426,12 +431,10 @@
 
     row_wide[...] = jnp.zeros((ROWS, 128), F32)
     lax.fori_loop(0, BLOCKS, student_block, 0)
-    row_send[0, 4:8] = fold_lanes(row_wide[...])
+    row_start(3, fold_lanes(row_wide[...]))
     col_finish(0)
-    row_send[0, 0:4] = row_pass()
-    row_start(0)
+    row_start(0, row_pass())
     student_turned[...] = student_unit[...].astype(F32).T.astype(BF16)
-    row_ring(0)
 
     def turn_block(block, carry):
         cols = columns(block)
@@ -439,9 +442,8 @@
         return carry
 
     lax.fori_loop(0, BLOCKS, turn_block, 0)
-    sums = row_finish(0)
-    row_scale = 1.0 / (ALL_ROWS * sums[0:4])
-    student_total = sums[4:8]
+    student_total = row_finish(3)
+    row_scale = 1.0 / (ALL_ROWS * row_finish(0))
 
     row_wide[...] = lane_broadcast(row_scale)
     col_pass()
@@ -459,44 +461,42 @@
     lax.fori_loop(0, ROWS // 64, soft_rows, 0)
     unit_matmul(soft_half, pl.ds(0, ROWS))
     col_finish(1)
-    row_send[1, 0:4] = row_pass()
-    row_start(1)
-    row_ring(1)
-    unit_x(0)
+    row_start(1, row_pass())
+    soft_x()
     row_scale = 1.0 / (ALL_ROWS * row_finish(1))
 
     row_wide[...] = lane_broadcast(row_scale)
     col_pass()
     col_start(2)
-    unit_far(0)
-    unit_near(0)
+    soft_ring()
     soft_own = unit_own(0)
     col_finish(2)
-    row_send[2, 0:4] = target_pass()
-    row_start(2)
-    unit_matmul(target_half, pl.ds(0, ROWS))
-    unit_x(1)
-    unit_far(1)
-    row_ring(2)
+    row_start(2, target_pass())
+    unit_matmul(target_half, other)
+    unit_x()
+    unit_far(across, FAR)
+    unit_matmul(target_half, mine)
+    unit_send[1, mine, :] = unit_part[mine, :].astype(BF16)
+    unit_far(here, 0)
     row_wide[...] = unit_part[:, :128] * student_unit[:, :128].astype(F32) + unit_part[:, 128:] * student_unit[
         :, 128:
     ].astype(F32)
     loss_row[0] = fold_lanes(row_wide[...])
     remote(loss_row.at[0], loss_pair, loss_sem.at[0], partner_x).start()
-    unit_near(1)
+    unit_near()
     target_own = unit_own(1)
     landed(loss_pair, loss_sem.at[0])
     loss_row[1] = loss_row[0] + loss_pair[...]
     loss_recv[RING - 1] = loss_row[1]
 
-    def loss_send(step, carry):
+    def loss_ring(step, carry):
         remote(
             loss_row.at[1], loss_recv.at[RING - 1 - step], loss_sem.at[1], (grp, here + z_peer(step))
         ).start()
         return carry
 
-    lax.fori_loop(1, RING, loss_send, 0)
-    soft_unit = unit_finish(0, soft_own)
+    lax.fori_loop(1, RING, loss_ring, 0)
+    soft_unit = soft_finish(soft_own)
     row_scale = 1.0 / (ALL_ROWS * row_finish(2))
     row_wide[...] = lane_broadcast((ALL_ROWS / STUDENT_TEMP) * row_scale)
 
@@ -548,22 +548,20 @@
     left(loss_recv.at[pl.ds(0, RING - 1)], loss_sem.at[1])
     loss_here = jnp.sum(jnp.log(student_total) - agreement) * (1.0 / ALL_ROWS)
 
-    high = loss_here.astype(BF16).astype(F32)
-    middle = (loss_here - high).astype(BF16).astype(F32)
-    low = loss_here - high - middle
-    place = lax.broadcasted_iota(jnp.int32, (16, 128), 0)
-    pieces = jnp.where(place == 0, high, jnp.where(place == 1, middle, jnp.where(place == 2, low, 0.0)))
-    dot_send[0:TILES] = dots[...].astype(BF16)
-    dot_send[TILES : TILES + 16] = pieces.astype(BF16)
+    loss_send[...] = jnp.full((1, 128), loss_here, F32)
+    loss_all[GRP - 1] = loss_send[...]
+    dot_send[...] = dots[...].astype(BF16)
     dot_recv[GRP - 1] = dot_send[...]
 
     def dot_start(step, carry):
-        remote(dot_send, dot_recv.at[GRP - 1 - step], dot_sem, (grp_peer(step), proto)).start()
+        device = (grp_peer(step), proto)
+        remote(dot_send, dot_recv.at[GRP - 1 - step], dot_sem, device).start()
+        remote(loss_send, loss_all.at[GRP - 1 - step], loss_sem.at[2], device).start()
         return carry
 
     lax.fori_loop(1, GRP, dot_start, 0)
 
-    target_unit = unit_finish(1, target_own)
+    target_unit = unit_finish(target_own)
     my_rows = own_rows(here + z)
     unit_grad = soft_unit - target_unit * row_wide[my_rows, 0:1]
     wide, scaling = unit_rows(student_in[my_rows, :])
@@ -586,18 +584,24 @@
     near_steps(lambda step: out_send(step, here, out_sem.at[0]))
     forward(z)
 
-    dot_arrivals = dot_recv.at[pl.ds(0, GRP - 1)]
-    landed(dot_arrivals, dot_sem)
-    total = jnp.zeros((TILES + 16, 128), F32)
-    for index in range(GRP):
-        total = total + dot_recv[lax.rem(index + GRP - 1 - grp + GRP, GRP)].astype(F32)
-    dots[...] = total[0:TILES]
-    loss_out[...] = total[TILES : TILES + 1] + total[TILES + 1 : TILES + 2] + total[TILES + 2 : TILES + 3]
-    left(dot_arrivals, dot_sem)
-
     near_out = student_out.at[pl.ds(0, 2 * NEAR * OWN)]
     landed(near_out, out_sem.at[0])
     near_steps(lambda step: forward(z_peer(step)))
+
+    dot_arrivals = dot_recv.at[pl.ds(0, GRP - 1)]
+    landed(dot_arrivals, dot_sem)
+    total = dot_recv[0].astype(F32)
+    for slot in range(1, GRP):
+        total = total + dot_recv[slot].astype(F32)
+    dots[...] = total
+    left(dot_arrivals, dot_sem)
+    loss_arrivals = loss_all.at[pl.ds(0, GRP - 1)]
+    landed(loss_arrivals, loss_sem.at[2])
+    total = jnp.zeros((1, 128), F32)
+    for index in range(GRP):
+        total = total + loss_all[lax.rem(index + GRP - 1 - grp + GRP, GRP)]
+    loss_out[...] = total
+    left(loss_arrivals, loss_sem.at[2])
 
     def term_finish(block, carry):
         cols = columns(block, TERM_BLOCK)
@@ -657,13 +661,13 @@
             vmem((ITERS, TILES, 128), BF16),
             vmem((ITERS, GRP, TILES, 128), BF16),
             vmem((TILES, 128), F32),
-            vmem((ITERS, 8, 128), F32),
-            vmem((ITERS, 2, 8, 128), F32),
-            vmem((ITERS, RING, 8, 128), F32),
-            vmem((ITERS, 2 * FAR, 8, 128), F32),
+            vmem((ITERS + 1, 4, 128), F32),
+            vmem((ITERS + 1, 2 * RING, 4, 128), F32),
             vmem((2, 4, 128), F32),
             vmem((4, 128), F32),
             vmem((RING, 4, 128), F32),
+            vmem((1, 128), F32),
+            vmem((GRP, 1, 128), F32),
             vmem((ROWS, WIDTH), F32),
             vmem((2, ROWS, WIDTH), BF16),
             vmem((2, HALF_ROWS, WIDTH), BF16),
@@ -676,14 +680,12 @@
             vmem((TERM_BLOCKS, CHIPS, SHARE, TERM_BLOCK), BF16),
             vmem((TERM_BLOCKS, CHIPS - 1, SHARE, TERM_BLOCK), BF16),
             vmem((TILES, 128), F32),
-            vmem((TILES + 16, 128), BF16),
-            vmem((GRP, TILES + 16, 128), BF16),
+            vmem((TILES, 128), BF16),
+            vmem((GRP, TILES, 128), BF16),
             dma((2 + BLOCKS,)),
             dma((ITERS, 2)),
-            dma((ITERS, 2)),
-            dma((ITERS, 2)),
-            dma((ITERS, 2)),
-            dma((2, 2)),
+            dma((ITERS + 1, 2)),
+            dma((3, 2)),
             dma((2, 2)),
             dma((2, 2)),
             dma((3, 2)),

time: 97.7 us -> 92.4 us (0.946)
  the two profiles are of different devices: /device:TPU:1 before, /device:TPU:2 now
where the time goes in v4:
time: 92.4 us; the launch traced here: 92.2 us
  Pallas kernels  88.5 us (96%)
  between operations  2.33 us (3%)
  local copies, waits for them, and re-layouts  1.36 us (1%)
    pallas_call x1, Pallas kernels, per_device(): pl.pallas_call(kernel, out_shape=(vmem((SHARE, COLS), BF16), vmem((ROWS,...  88.5 us

profile of v4, /device:TPU:2, one launch (start us, length us, event | category | flops | bytes accessed | tf_op | source)
XLA Modules:
  0.0 92.2 jit_solution(10157323296546087792)
XLA Ops:
  0.6 88.5 %sinkhorn_step.1 = (bf16[16,4096]{1,0:T(8,128)(2,1)S(1)}, bf16[512,256]{1,0:T(8,128)(2,1)S(1)}, f32[1,128]{1,0:T(1,128)}) custom-call(bf16[512,256]{1,0:T(8,128)(2,1)} %teacher_hbm.1, bf16[512,256]{1,0:T(8,128)(2,1)} %student_hbm.1, bf16[256,4096]{1,0:T(8,128)(2,1)} %proto_hbm.1), custom_call_target="tpu_custom_call" | custom-call | tf_op jit(solution)/shard_map/sinkhorn_step/pallas_call | solution.py:637
  89.2 0.7 copy.9
  89.8 0.7 copy.10

commit v5 on v4

--- a/solution.py
+++ b/solution.py
@@ -31,8 +31,9 @@
 TERM_BLOCK = 512
 TERM_BLOCKS = COLS // TERM_BLOCK
 HALF_ROWS = ROWS // 2
-NEAR = 5
+NEAR = 4
 FAR = RING - 1 - 2 * NEAR
+LAG = 3
 SHARE = WIDTH // GRP
 CHIPS = 8
 OWN = ROWS // (2 * RING)
@@ -79,10 +80,8 @@
     col_scale,
     row_send,
     row_recv,
-    loss_row,
-    loss_pair,
-    loss_recv,
     loss_send,
+    loss_proto,
     loss_all,
     unit_part,
     unit_send,
@@ -244,23 +243,11 @@
 
     PEERS = 2 * RING - 1
 
-    def ring_order(slots):
-        total = slots[lax.rem(RING - 1 - z + RING, RING)]
-        for index in range(1, RING):
-            total = total + slots[lax.rem(index + RING - 1 - z + RING, RING)]
-        return total
-
-    def row_start(turn, sums):
-        row_send[turn] = sums
-        row_recv[turn, PEERS] = sums
+    def spread(source, slots, sem):
+        slots[PEERS] = source[...]
 
         def send(step, base, offset):
-            remote(
-                row_send.at[turn],
-                row_recv.at[turn, PEERS - offset - step],
-                row_sem.at[turn],
-                (grp, base + z_peer(step)),
-            ).start()
+            remote(source, slots.at[PEERS - offset - step], sem, (grp, base + z_peer(step))).start()
 
         def four(step, carry):
             for base, offset in ((here, 0), (across, RING)):
@@ -273,17 +260,23 @@
         lax.fori_loop(1, RING // 2, four, 0)
         send(0, across, RING)
 
-    def row_finish(turn):
-        arrivals = row_recv.at[turn, pl.ds(0, PEERS)]
-        landed(arrivals, row_sem.at[turn])
+    def gathered(slots, sem):
+        arrivals = slots.at[pl.ds(0, PEERS)]
+        landed(arrivals, sem)
         total = None
         for index in range(RING):
             slot = lax.rem(index + RING - 1 - z + RING, RING)
-            own = row_recv[turn, RING + slot]
-            other = row_recv[turn, slot]
-            total = own + other if total is None else total + (own + other)
-        left(arrivals, row_sem.at[turn])
+            pair = slots[RING + slot] + slots[slot]
+            total = pair if total is None else total + pair
+        left(arrivals, sem)
         return total
+
+    def row_start(turn, sums):
+        row_send[turn] = sums
+        spread(row_send.at[turn], row_recv.at[turn], row_sem.at[turn])
+
+    def row_finish(turn):
+        return gathered(row_recv.at[turn], row_sem.at[turn])
 
     def row_pass():
         def rows_of(block, carry):
@@ -297,9 +290,9 @@
         lax.fori_loop(0, ROWS // 64, rows_of, 0)
         return fold_lanes(row_wide[...])
 
-    def target_pass():
+    def target_pass(first):
         def rows_of(block, carry):
-            rows = pl.ds(pl.multiple_of(block * 64, 64), 64)
+            rows = pl.ds(pl.multiple_of(first + block * 64, 64), 64)
             partial = jnp.zeros((64, 128), F32)
             for tile in range(TILES):
                 cols = pl.ds(tile * 128, 128)
@@ -309,8 +302,7 @@
             row_wide[rows, :] = partial
             return carry
 
-        lax.fori_loop(0, ROWS // 64, rows_of, 0)
-        return fold_lanes(row_wide[...])
+        lax.fori_loop(0, HALF_ROWS // 64, rows_of, 0)
 
     def col_pass():
         def block_of(block, carry):
@@ -336,82 +328,46 @@
     def own_rows(index):
         return pl.ds(pl.multiple_of(index * OWN, OWN), OWN)
 
-    ring_rows = pl.ds(0, (RING - 1) * OWN)
+    far_rows = pl.ds(0, FAR * OWN)
     near_rows = pl.ds(0, (2 * NEAR + 1) * OWN)
 
-    def soft_x():
-        unit_send[0, other, :] = unit_part[other, :].astype(BF16)
-        remote(unit_send.at[0, other], unit_pair.at[0], unit_x_sem.at[0], partner_x).start()
-
-    def soft_ring():
-        landed(unit_pair.at[0], unit_x_sem.at[0])
-        total = unit_part[mine, :] + unit_pair[0].astype(F32)
-        unit_share[0] = total.astype(BF16)
-
-        def send(step, carry):
-            peer = z_peer(step)
-            remote(
-                unit_share.at[0, own_rows(peer)], unit_recv.at[0, step - 1], unit_z_sem.at[0], (grp, here + peer)
-            ).start()
-            return carry
-
-        lax.fori_loop(1, RING, send, 0)
-
-    def soft_finish(total):
-        landed(unit_recv.at[0, pl.ds(0, RING - 1)], unit_z_sem.at[0])
-        for slot in range(RING - 1):
-            total = total + unit_recv[0, slot].astype(F32)
-        left(unit_pair.at[0], unit_x_sem.at[0])
-        left(unit_share.at[0, ring_rows], unit_z_sem.at[0])
-        return total
-
-    def unit_x():
-        unit_send[1, other, :] = unit_part[other, :].astype(BF16)
-
-        def send(step, carry):
-            owner = lax.rem(z + step + RING - NEAR, RING)
-            remote(
-                unit_send.at[1, own_rows(across + owner)],
-                unit_pair.at[1, own_rows(owner)],
-                unit_x_sem.at[1],
-                partner_x,
-            ).start()
-            return carry
-
-        lax.fori_loop(0, 2 * NEAR + 1, send, 0)
-
-    def unit_far(base, offset):
-        def to_far(step):
-            peer = z_peer(step)
-            slot = offset + 2 * NEAR + RING // 2 + FAR // 2 - step
-            remote(
-                unit_send.at[1, own_rows(base + peer)], unit_recv.at[1, slot], unit_z_sem.at[1], (grp, base + peer)
-            ).start()
-
-        far_steps(to_far)
-
-    def unit_near():
-        landed(unit_pair.at[1, near_rows], unit_x_sem.at[1])
-
-        def to_near(step):
+    def unit_x(part):
+        unit_send[part] = unit_part[other, :].astype(BF16)
+
+        def send(sem):
+            def visit(step, carry):
+                rows = own_rows(z_peer(step))
+                remote(unit_send.at[part, rows], unit_pair.at[part, rows], sem, partner_x).start()
+                return carry
+
+            return visit
+
+        lax.fori_loop(NEAR + 1, RING - NEAR, send(unit_x_sem.at[part, 0]), 0)
+        lax.fori_loop(RING - NEAR, RING + NEAR + 1, send(unit_x_sem.at[part, 1]), 0)
+
+    def unit_ring(part):
+        def send(step):
             peer = z_peer(step)
             rows = own_rows(peer)
-            total = unit_part[own_rows(here + peer), :] + unit_pair[1, rows, :].astype(F32)
-            unit_share[1, rows, :] = total.astype(BF16)
-            slot = step - 1 - NEAR * lax.div(step, RING // 2)
-            remote(unit_share.at[1, rows], unit_recv.at[1, slot], unit_z_sem.at[1], (grp, here + peer)).start()
-
-        near_steps(to_near)
-
-    def unit_own(part):
+            total = unit_part[own_rows(here + peer), :] + unit_pair[part, rows, :].astype(F32)
+            unit_share[part, rows, :] = total.astype(BF16)
+            remote(
+                unit_share.at[part, rows], unit_recv.at[part, step - 1], unit_z_sem.at[part], (grp, here + peer)
+            ).start()
+
+        landed(unit_pair.at[part, far_rows], unit_x_sem.at[part, 0])
+        far_steps(send)
+        landed(unit_pair.at[part, near_rows], unit_x_sem.at[part, 1])
+        near_steps(send)
         return unit_part[own_rows(here + z), :] + unit_pair[part, own_rows(z), :].astype(F32)
 
-    def unit_finish(total):
-        landed(unit_recv.at[1], unit_z_sem.at[1])
-        for slot in range(2 * NEAR + 2 * FAR):
-            total = total + unit_recv[1, slot].astype(F32)
-        left(unit_pair.at[1, near_rows], unit_x_sem.at[1])
-        left(unit_recv.at[1], unit_z_sem.at[1])
+    def unit_finish(part, total):
+        landed(unit_recv.at[part], unit_z_sem.at[part])
+        for slot in range(RING - 1):
+            total = total + unit_recv[part, slot].astype(F32)
+        left(unit_pair.at[part, far_rows], unit_x_sem.at[part, 0])
+        left(unit_pair.at[part, near_rows], unit_x_sem.at[part, 1])
+        left(unit_recv.at[part], unit_z_sem.at[part])
         return total
 
     col_start(0)
@@ -462,42 +418,30 @@
     unit_matmul(soft_half, pl.ds(0, ROWS))
     col_finish(1)
     row_start(1, row_pass())
-    soft_x()
+    unit_x(0)
     row_scale = 1.0 / (ALL_ROWS * row_finish(1))
 
     row_wide[...] = lane_broadcast(row_scale)
     col_pass()
     col_start(2)
-    soft_ring()
-    soft_own = unit_own(0)
+    soft_own = unit_ring(0)
     col_finish(2)
-    row_start(2, target_pass())
+    target_pass((1 - x_lo) * HALF_ROWS)
     unit_matmul(target_half, other)
-    unit_x()
-    unit_far(across, FAR)
+    unit_x(1)
+    target_pass(x_lo * HALF_ROWS)
+    row_start(2, fold_lanes(row_wide[...]))
     unit_matmul(target_half, mine)
-    unit_send[1, mine, :] = unit_part[mine, :].astype(BF16)
-    unit_far(here, 0)
+    target_own = unit_ring(1)
     row_wide[...] = unit_part[:, :128] * student_unit[:, :128].astype(F32) + unit_part[:, 128:] * student_unit[
         :, 128:
     ].astype(F32)
-    loss_row[0] = fold_lanes(row_wide[...])
-    remote(loss_row.at[0], loss_pair, loss_sem.at[0], partner_x).start()
-    unit_near()
-    target_own = unit_own(1)
-    landed(loss_pair, loss_sem.at[0])
-    loss_row[1] = loss_row[0] + loss_pair[...]
-    loss_recv[RING - 1] = loss_row[1]
-
-    def loss_ring(step, carry):
-        remote(
-            loss_row.at[1], loss_recv.at[RING - 1 - step], loss_sem.at[1], (grp, here + z_peer(step))
-        ).start()
-        return carry
-
-    lax.fori_loop(1, RING, loss_ring, 0)
-    soft_unit = soft_finish(soft_own)
+    agreement = fold_lanes(row_wide[...])
+    soft_unit = unit_finish(0, soft_own)
     row_scale = 1.0 / (ALL_ROWS * row_finish(2))
+    share = jnp.log(student_total) * (1.0 / (2 * RING)) - (ALL_ROWS / STUDENT_TEMP) * row_scale * agreement
+    loss_send[0] = jnp.full((1, 128), jnp.sum(share) * (1.0 / ALL_ROWS), F32)
+    spread(loss_send.at[0], loss_proto, loss_sem.at[0])
     row_wide[...] = lane_broadcast((ALL_ROWS / STUDENT_TEMP) * row_scale)
 
     def core_copy(block):
@@ -534,34 +478,25 @@
         for tile in range(TERM_BLOCK // 128):
             dots[pl.ds(block * (TERM_BLOCK // 128) + tile, 1), :] = total[:, tile * 128 : (tile + 1) * 128]
 
-        @pl.when(block > 0)
+        @pl.when(block >= LAG)
         def _():
-            term_ring(block - 1)
+            term_ring(block - LAG)
 
         return carry
 
     lax.fori_loop(0, TERM_BLOCKS, term_block, 0)
-    term_ring(TERM_BLOCKS - 1)
-    landed(loss_recv.at[pl.ds(0, RING - 1)], loss_sem.at[1])
-    agreement = (ALL_ROWS / STUDENT_TEMP) * row_scale * ring_order(loss_recv)
-    left(loss_pair, loss_sem.at[0])
-    left(loss_recv.at[pl.ds(0, RING - 1)], loss_sem.at[1])
-    loss_here = jnp.sum(jnp.log(student_total) - agreement) * (1.0 / ALL_ROWS)
-
-    loss_send[...] = jnp.full((1, 128), loss_here, F32)
-    loss_all[GRP - 1] = loss_send[...]
+    lax.fori_loop(TERM_BLOCKS - LAG, TERM_BLOCKS, lambda block, carry: (term_ring(block), carry)[1], 0)
+
     dot_send[...] = dots[...].astype(BF16)
     dot_recv[GRP - 1] = dot_send[...]
 
     def dot_start(step, carry):
-        device = (grp_peer(step), proto)
-        remote(dot_send, dot_recv.at[GRP - 1 - step], dot_sem, device).start()
-        remote(loss_send, loss_all.at[GRP - 1 - step], loss_sem.at[2], device).start()
+        remote(dot_send, dot_recv.at[GRP - 1 - step], dot_sem, (grp_peer(step), proto)).start()
         return carry
 
     lax.fori_loop(1, GRP, dot_start, 0)
 
-    target_unit = unit_finish(target_own)
+    target_unit = unit_finish(1, target_own)
     my_rows = own_rows(here + z)
     unit_grad = soft_unit - target_unit * row_wide[my_rows, 0:1]
     wide, scaling = unit_rows(student_in[my_rows, :])
@@ -572,21 +507,30 @@
         rows = student_out.at[my_rows]
         remote(rows, rows, sem, (grp, base + z_peer(step))).start()
 
-    def out_far(step):
-        out_send(step, across, out_sem.at[1])
-        out_send(step, here, out_sem.at[1])
-
     def forward(owner):
         rows = student_out.at[own_rows(here + owner)]
         remote(rows, rows, out_sem.at[2], partner_x).start()
 
-    far_steps(out_far)
+    far_steps(lambda step: out_send(step, here, out_sem.at[1]))
     near_steps(lambda step: out_send(step, here, out_sem.at[0]))
     forward(z)
 
+    loss_send[1] = gathered(loss_proto, loss_sem.at[0])
+    loss_all[GRP - 1] = loss_send[1]
+
+    def loss_start(step, carry):
+        remote(loss_send.at[1], loss_all.at[GRP - 1 - step], loss_sem.at[1], (grp_peer(step), proto)).start()
+        return carry
+
+    lax.fori_loop(1, GRP, loss_start, 0)
+
     near_out = student_out.at[pl.ds(0, 2 * NEAR * OWN)]
+    far_out = student_out.at[pl.ds(0, FAR * OWN)]
+    passed_out = student_out.at[pl.ds(0, RING * OWN)]
     landed(near_out, out_sem.at[0])
     near_steps(lambda step: forward(z_peer(step)))
+    landed(far_out, out_sem.at[1])
+    far_steps(lambda step: forward(z_peer(step)))
 
     dot_arrivals = dot_recv.at[pl.ds(0, GRP - 1)]
     landed(dot_arrivals, dot_sem)
@@ -596,12 +540,12 @@
     dots[...] = total
     left(dot_arrivals, dot_sem)
     loss_arrivals = loss_all.at[pl.ds(0, GRP - 1)]
-    landed(loss_arrivals, loss_sem.at[2])
+    landed(loss_arrivals, loss_sem.at[1])
     total = jnp.zeros((1, 128), F32)
     for index in range(GRP):
         total = total + loss_all[lax.rem(index + GRP - 1 - grp + GRP, GRP)]
     loss_out[...] = total
-    left(loss_arrivals, loss_sem.at[2])
+    left(loss_arrivals, loss_sem.at[1])
 
     def term_finish(block, carry):
         cols = columns(block, TERM_BLOCK)
@@ -622,9 +566,6 @@
 
     lax.fori_loop(0, TERM_BLOCKS, term_finish, 0)
 
-    far_out = student_out.at[pl.ds(0, 2 * FAR * OWN)]
-    passed_out = student_out.at[pl.ds(0, (2 * NEAR + 1) * OWN)]
-    landed(far_out, out_sem.at[1])
     landed(passed_out, out_sem.at[2])
     left(near_out, out_sem.at[0])
     left(far_out, out_sem.at[1])
@@ -663,16 +604,14 @@
             vmem((TILES, 128), F32),
             vmem((ITERS + 1, 4, 128), F32),
             vmem((ITERS + 1, 2 * RING, 4, 128), F32),
-            vmem((2, 4, 128), F32),
-            vmem((4, 128), F32),
-            vmem((RING, 4, 128), F32),
-            vmem((1, 128), F32),
+            vmem((2, 1, 128), F32),
+            vmem((2 * RING, 1, 128), F32),
             vmem((GRP, 1, 128), F32),
             vmem((ROWS, WIDTH), F32),
-            vmem((2, ROWS, WIDTH), BF16),
             vmem((2, HALF_ROWS, WIDTH), BF16),
             vmem((2, HALF_ROWS, WIDTH), BF16),
-            vmem((2, 2 * NEAR + 2 * FAR, OWN, WIDTH), BF16),
+            vmem((2, HALF_ROWS, WIDTH), BF16),
+            vmem((2, RING - 1, OWN, WIDTH), BF16),
             vmem((CHIPS, 2, SHARE, TERM_BLOCK), F32),
             vmem((TERM_BLOCKS, CHIPS, SHARE, TERM_BLOCK), BF16),
             vmem((TERM_BLOCKS, CHIPS, SHARE, TERM_BLOCK), BF16),
@@ -685,8 +624,8 @@
             dma((2 + BLOCKS,)),
             dma((ITERS, 2)),
             dma((ITERS + 1, 2)),
-            dma((3, 2)),
             dma((2, 2)),
+            dma((2, 2, 2)),
             dma((2, 2)),
             dma((3, 2)),
             dma((TERM_BLOCKS, 2)),

time: 92.4 us -> 88.5 us (0.958)
  the two profiles are of different devices: /device:TPU:2 before, /device:TPU:1 now
where the time goes in v5:
time: 88.5 us; the launch traced here: 88.4 us
  Pallas kernels  84.7 us (96%)
  between operations  2.33 us (3%)
  local copies, waits for them, and re-layouts  1.36 us (2%)
    pallas_call x1, Pallas kernels, per_device(): pl.pallas_call(kernel, out_shape=(vmem((SHARE, COLS), BF16), vmem((ROWS,...  84.7 us

profile of v5, /device:TPU:1, one launch (start us, length us, event | category | flops | bytes accessed | tf_op | source)
XLA Modules:
  0.0 88.4 jit_solution(9365700800213208308)
XLA Ops:
  0.6 84.7 %sinkhorn_step.1 = (bf16[16,4096]{1,0:T(8,128)(2,1)S(1)}, bf16[512,256]{1,0:T(8,128)(2,1)S(1)}, f32[1,128]{1,0:T(1,128)}) custom-call(bf16[512,256]{1,0:T(8,128)(2,1)} %teacher_hbm.1, bf16[512,256]{1,0:T(8,128)(2,1)} %student_hbm.1, bf16[256,4096]{1,0:T(8,128)(2,1)} %proto_hbm.1), custom_call_target="tpu_custom_call" | custom-call | tf_op jit(solution)/shard_map/sinkhorn_step/pallas_call | solution.py:578
  85.3 0.7 copy.9
  86.0 0.7 copy.10

commit v6 on v5

--- a/solution.py
+++ b/solution.py
@@ -28,12 +28,12 @@
 BLOCK = 512
 BLOCKS = COLS // BLOCK
 TILES = COLS // 128
-TERM_BLOCK = 512
+TERM_BLOCK = 1024
 TERM_BLOCKS = COLS // TERM_BLOCK
 HALF_ROWS = ROWS // 2
 NEAR = 4
 FAR = RING - 1 - 2 * NEAR
-LAG = 3
+LAG = 1
 SHARE = WIDTH // GRP
 CHIPS = 8
 OWN = ROWS // (2 * RING)
@@ -290,9 +290,9 @@
         lax.fori_loop(0, ROWS // 64, rows_of, 0)
         return fold_lanes(row_wide[...])
 
-    def target_pass(first):
+    def target_pass():
         def rows_of(block, carry):
-            rows = pl.ds(pl.multiple_of(first + block * 64, 64), 64)
+            rows = pl.ds(pl.multiple_of(block * 64, 64), 64)
             partial = jnp.zeros((64, 128), F32)
             for tile in range(TILES):
                 cols = pl.ds(tile * 128, 128)
@@ -302,7 +302,7 @@
             row_wide[rows, :] = partial
             return carry
 
-        lax.fori_loop(0, HALF_ROWS // 64, rows_of, 0)
+        lax.fori_loop(0, ROWS // 64, rows_of, 0)
 
     def col_pass():
         def block_of(block, carry):
@@ -416,9 +416,9 @@
 
     lax.fori_loop(0, ROWS // 64, soft_rows, 0)
     unit_matmul(soft_half, pl.ds(0, ROWS))
+    unit_x(0)
     col_finish(1)
     row_start(1, row_pass())
-    unit_x(0)
     row_scale = 1.0 / (ALL_ROWS * row_finish(1))
 
     row_wide[...] = lane_broadcast(row_scale)
@@ -426,11 +426,10 @@
     col_start(2)
     soft_own = unit_ring(0)
     col_finish(2)
-    target_pass((1 - x_lo) * HALF_ROWS)
+    target_pass()
+    row_start(2, fold_lanes(row_wide[...]))
     unit_matmul(target_half, other)
     unit_x(1)
-    target_pass(x_lo * HALF_ROWS)
-    row_start(2, fold_lanes(row_wide[...]))
     unit_matmul(target_half, mine)
     target_own = unit_ring(1)
     row_wide[...] = unit_part[:, :128] * student_unit[:, :128].astype(F32) + unit_part[:, 128:] * student_unit[

time: 88.5 us -> 87.3 us (0.986)
  Pallas kernels: 84.7 us -> 83.4 us
    pallas_call x1, Pallas kernels: 84.7 us -> 83.4 us  [per_device(): pl.pallas_call(kernel, out_shape=(vmem((SHARE, COLS), BF16), vmem((ROWS,...]
where the time goes in v6:
time: 87.3 us; the launch traced here: 87.1 us
  Pallas kernels  83.4 us (96%)
  between operations  2.33 us (3%)
  local copies, waits for them, and re-layouts  1.36 us (2%)
    pallas_call x1, Pallas kernels, per_device(): pl.pallas_call(kernel, out_shape=(vmem((SHARE, COLS), BF16), vmem((ROWS,...  83.4 us

profile of v6, /device:TPU:1, one launch (start us, length us, event | category | flops | bytes accessed | tf_op | source)
XLA Modules:
  0.0 87.1 jit_solution(15331643170481977735)
XLA Ops:
  0.6 83.4 %sinkhorn_step.1 = (bf16[16,4096]{1,0:T(8,128)(2,1)S(1)}, bf16[512,256]{1,0:T(8,128)(2,1)S(1)}, f32[1,128]{1,0:T(1,128)}) custom-call(bf16[512,256]{1,0:T(8,128)(2,1)} %teacher_hbm.1, bf16[512,256]{1,0:T(8,128)(2,1)} %student_hbm.1, bf16[256,4096]{1,0:T(8,128)(2,1)} %proto_hbm.1), custom_call_target="tpu_custom_call" | custom-call | tf_op jit(solution)/shard_map/sinkhorn_step/pallas_call | solution.py:577
  84.1 0.7 copy.9
  84.7 0.7 copy.10

commit v7 on v6

--- a/solution.py
+++ b/solution.py
@@ -33,7 +33,9 @@
 HALF_ROWS = ROWS // 2
 NEAR = 4
 FAR = RING - 1 - 2 * NEAR
-LAG = 1
+GRP_STEPS = (6, 10, 7, 9, 2, 14, 5, 11, 8, 3, 13, 1, 15, 4, 12)
+CHIP_STEPS = (3, 5, 1, 7, 4, 2, 6)
+LAG = 2
 SHARE = WIDTH // GRP
 CHIPS = 8
 OWN = ROWS // (2 * RING)
@@ -196,8 +198,18 @@
         scaling = lax.rsqrt(jnp.sum(wide * wide, axis=1, keepdims=True) + EPSILON)
         return wide * scaling, scaling
 
+    def unit_all(features):
+        wide = features.astype(F32)
+        squares = wide * wide
+        high = squares.astype(BF16)
+        low = (squares - high.astype(F32)).astype(BF16)
+        ones = jnp.ones((WIDTH, 128), BF16)
+        total = jnp.dot(high, ones, preferred_element_type=F32) + jnp.dot(low, ones, preferred_element_type=F32)
+        scaling = lax.rsqrt(total + EPSILON)
+        return (wide * jnp.concatenate([scaling] * (WIDTH // 128), axis=1)).astype(BF16)
+
     loads[0].wait()
-    teacher_in[...] = unit_rows(teacher_in[...])[0].astype(BF16)
+    teacher_in[...] = unit_all(teacher_in[...])
 
     def teacher_block(block, carry):
         proto_load(block).wait()
@@ -224,13 +236,10 @@
         col_send[turn] = message
         col_recv[turn, GRP - 1] = message
 
-        def send(step, carry):
+        for step in GRP_STEPS:
             remote(
                 col_send.at[turn], col_recv.at[turn, GRP - 1 - step], col_sem.at[turn], (grp_peer(step), proto)
             ).start()
-            return carry
-
-        lax.fori_loop(1, GRP, send, 0)
 
     def col_finish(turn):
         arrivals = col_recv.at[turn, pl.ds(0, GRP - 1)]
@@ -372,7 +381,7 @@
 
     col_start(0)
     loads[1].wait()
-    student_unit[...] = unit_rows(student_in[...])[0].astype(BF16)
+    student_unit[...] = unit_all(student_in[...])
 
     def student_block(block, carry):
         cols = columns(block)
@@ -452,7 +461,7 @@
         term_mine[block] = total
         term_send[block] = total.astype(BF16)
 
-        def send(step, carry):
+        for step in CHIP_STEPS:
             peer = chip_peer(step)
             remote(
                 term_send.at[block, peer],
@@ -460,9 +469,6 @@
                 term_sem.at[block],
                 (peer * 2 + core, proto),
             ).start()
-            return carry
-
-        lax.fori_loop(1, CHIPS, send, 0)
 
     def term_block(block, carry):
         cols = columns(block, TERM_BLOCK)

time: 87.3 us -> 86.8 us (level)
  no operation moved by 1% of the time
where the time goes in v7:
time: 86.8 us; the launch traced here: 86.7 us
  Pallas kernels  83 us (96%)
  between operations  2.33 us (3%)
  local copies, waits for them, and re-layouts  1.36 us (2%)
    pallas_call x1, Pallas kernels, per_device(): pl.pallas_call(kernel, out_shape=(vmem((SHARE, COLS), BF16), vmem((ROWS,...  83 us

profile of v7, /device:TPU:1, one launch (start us, length us, event | category | flops | bytes accessed | tf_op | source)
XLA Modules:
  0.0 86.7 jit_solution(16446977045682608246)
XLA Ops:
  0.6 83.0 %sinkhorn_step.1 = (bf16[16,4096]{1,0:T(8,128)(2,1)S(1)}, bf16[512,256]{1,0:T(8,128)(2,1)S(1)}, f32[1,128]{1,0:T(1,128)}) custom-call(bf16[512,256]{1,0:T(8,128)(2,1)} %teacher_hbm.1, bf16[512,256]{1,0:T(8,128)(2,1)} %student_hbm.1, bf16[256,4096]{1,0:T(8,128)(2,1)} %proto_hbm.1), custom_call_target="tpu_custom_call" | custom-call | tf_op jit(solution)/shard_map/sinkhorn_step/pallas_call | solution.py:583
  83.6 0.7 copy.9
  84.3 0.7 copy.10
